TPU v7x, 128 devices: a whole 4x4x4 slice. The times are simulated.
128 devices in a mesh: grid: 8 (over x, core), mark: 16 (over z, y).
Axes of the slice: x: 4, y: 4, z: 4, core: 2. Of those that a mesh axis runs over, the one named last changes fastest.
Arguments:
- velocity: float32 [3, 256, 256, 256], P(None, 'grid', 'mark'), may hold values from -6 to 6
- pressure: float32 [256, 256, 256], P('grid', 'mark'), may hold values from -6 to 6
- cell_visc: float32 [256, 256, 256], P('grid', 'mark'), may hold values from 0.2 to 5
- cell_dens: float32 [256, 256, 256], P('grid', 'mark'), may hold values from 0.5 to 1.5
- block_brick: int32 [2048, 48], P(('grid', 'mark')), may hold values from 0 to 1023
- block_counts: int32 [128, 16], P(('grid', 'mark')), may hold values from 0 to 48, as said below
- positions: float32 [2048, 3, 48, 256], P(('grid', 'mark')), may hold values from 0 to 1
- start_visc: float32 [2048, 48, 256], P(('grid', 'mark')), may hold values from 0.2 to 5
- marker_dens: float32 [2048, 48, 256], P(('grid', 'mark')), may hold values from 0.5 to 1.5
Outputs:
- velocity_next: float32 [3, 256, 256, 256], P(None, 'grid', 'mark')
- pressure_next: float32 [256, 256, 256], P('grid', 'mark')
- visc_next: float32 [256, 256, 256], P('grid', 'mark')
- dens_next: float32 [256, 256, 256], P('grid', 'mark')
- marker_visc: float32 [2048, 48, 256], P(('grid', 'mark'))
Inputs may be any that keep to these rules, and one draw needn't show every extreme that they name: `block_counts`: entry q of a marker device's row counts its live slots toward the grid device of mark index q in its group; in every group some grid device gets exactly 48 live slots from every marker device. `block_brick`: dead slots name bricks too.
All inputs are finite; a program needn't handle non-finite values.
Results may differ from a plain program's by a relative error of at most 0.0003.
Values sent between devices are 32-bit elements; how exact they have to be, the bound alone decides.
A program may use at most 128 MiB of HBM per device.

v0:
```python
import jax
import jax.numpy as jnp
from jax import lax
from jax.sharding import PartitionSpec as P

ITERS = 4


relax_weight = 0.6
pressure_rate = 0.25
gravity = 1.0
strain_scale = 0.5


def extended(value, sides, width):
    for axis, dim in sides:
        size, length = (lax.axis_size(axis), value.shape[dim])
        up = [(i, (i + 1) % size) for i in range(size - 1)]
        down = [(j, i) for i, j in up]
        last = lax.slice_in_dim(value, length - width, length, axis=dim)
        initial = lax.slice_in_dim(value, 0, width, axis=dim)
        before = lax.ppermute(last, axis, up)
        after = lax.ppermute(initial, axis, down)
        value = jnp.concatenate([before, value, after], axis=dim)
    return value


def neighbours(padded):
    centre = padded[1:-1, 1:-1, 1:-1]
    return (
        centre,
        [
            padded[2:, 1:-1, 1:-1],
            padded[:-2, 1:-1, 1:-1],
            padded[1:-1, 2:, 1:-1],
            padded[1:-1, :-2, 1:-1],
            padded[1:-1, 1:-1, 2:],
            padded[1:-1, 1:-1, :-2],
        ],
    )


def relax_sweep(padded_velocity, padded_pressure, padded_visc, density):
    viscosity, visc_near = neighbours(padded_visc)
    couplings = [0.5 * (viscosity + nearby) for nearby in visc_near]
    diagonal = sum(couplings)
    pressure, pressure_near = neighbours(padded_pressure)
    divergence = jnp.zeros_like(pressure)
    updated = []
    for component in range(3):
        current, current_near = neighbours(padded_velocity[component])
        laplace = sum(
            (weight * (nearby - current) for weight, nearby in zip(couplings, current_near))
        )
        forcing = laplace - (pressure - pressure_near[2 * component + 1])
        if component == 2:
            forcing = forcing - gravity * density
        updated.append(current + relax_weight * forcing / diagonal)
        divergence = divergence + current_near[2 * component] - current
    return (jnp.stack(updated), pressure - pressure_rate * viscosity * divergence)


def kernel(fraction, number_cells):
    position = fraction * number_cells
    centres = jnp.arange(number_cells, dtype=jnp.float32) + 0.5
    offset = position[:, None, :] - centres[None, :, None]
    gaussian = jnp.exp(-offset * offset)
    weights = gaussian / jnp.sum(gaussian, axis=1, keepdims=True)
    slopes = weights * (2.0 * jnp.sum(weights * offset, axis=1, keepdims=True) - 2.0 * offset)
    return (weights, slopes)


def marker_blocks(bricks, positions, start_visc, density, live_slots):
    highest = lax.Precision.HIGHEST
    blocks = bricks.shape[0]
    markers = positions.shape[-1]
    across_x, slope_x = kernel(positions[0], 4)
    across_y, slope_y = kernel(positions[1], 4)
    across_z, slope_z = kernel(positions[2], 8)
    values = bricks.reshape(blocks, 48, 8)
    interpolated = jnp.einsum("kcz,kzm->kcm", values, across_z, precision=highest).reshape(
        blocks, 3, 4, 4, markers
    )
    rising = jnp.einsum("kcz,kzm->kcm", values, slope_z, precision=highest).reshape(
        blocks, 3, 4, 4, markers
    )
    plane_xy = across_x[:, :, None, :] * across_y[:, None, :, :]
    plane_dx = slope_x[:, :, None, :] * across_y[:, None, :, :]
    plane_dy = across_x[:, :, None, :] * slope_y[:, None, :, :]
    grad_x = jnp.sum(interpolated * plane_dx[:, None], axis=(2, 3))
    grad_y = jnp.sum(interpolated * plane_dy[:, None], axis=(2, 3))
    grad_z = jnp.sum(rising * plane_xy[:, None], axis=(2, 3))
    normal = grad_x[:, 0] ** 2 + grad_y[:, 1] ** 2 + grad_z[:, 2] ** 2
    shear_xy = 0.5 * (grad_y[:, 0] + grad_x[:, 1])
    shear_xz = 0.5 * (grad_z[:, 0] + grad_x[:, 2])
    shear_yz = 0.5 * (grad_z[:, 1] + grad_y[:, 2])
    invariant = 0.5 * normal + shear_xy**2 + shear_xz**2 + shear_yz**2
    weakened = start_visc * jnp.exp(-jnp.log(1.0 + invariant / (strain_scale * strain_scale)) / 3.0)
    marker_visc = jnp.where(live_slots[:, None], weakened, 0.0)
    filled = jnp.broadcast_to(live_slots[:, None], weakened.shape).astype(jnp.float32)
    carried = jnp.stack([filled, filled * jnp.log(weakened), filled * density], axis=1)
    spread = (carried[:, :, None, None, :] * plane_xy[:, None]).reshape(blocks, 48, markers)
    moments = jnp.einsum("kcm,kzm->kcz", spread, across_z, precision=highest).reshape(blocks, 384)
    return (marker_visc, moments)


def per_device(
    velocity,
    pressure,
    cell_visc,
    cell_dens,
    block_brick,
    block_counts,
    positions,
    start_visc,
    marker_dens,
):
    highest = lax.Precision.HIGHEST
    size_x, size_y, size_z = cell_visc.shape
    near_visc = jnp.pad(
        extended(cell_visc, (("grid", 0), ("mark", 1)), 1), ((0, 0), (0, 0), (1, 1))
    )
    unknowns = jnp.concatenate([velocity, pressure[None]], axis=0)
    for iteration in range(ITERS):
        padded = jnp.pad(
            extended(unknowns, (("grid", 1), ("mark", 2)), 1), ((0, 0), (0, 0), (0, 0), (1, 1))
        )
        velocity_now, pressure_now = relax_sweep(padded[:3], padded[3], near_visc, cell_dens)
        unknowns = jnp.concatenate([velocity_now, pressure_now[None]], axis=0)
    bricks = (
        velocity.reshape(3, size_x // 4, 4, size_y // 4, 4, size_z // 8, 8)
        .transpose(1, 3, 5, 0, 2, 4, 6)
        .reshape(-1, 384)
    )
    owners = lax.axis_size("mark")
    whole_slab = lax.all_gather(bricks, "mark", axis=0, tiled=True)
    slab_rows = jnp.arange(owners, dtype=jnp.int32)[:, None] * bricks.shape[0] + block_brick
    fetched = whole_slab[slab_rows]
    live_slots = (
        jnp.arange(block_brick.shape[1], dtype=jnp.int32)[None, :] < block_counts[0][:, None]
    )

    def owner_work(inputs):
        received, places, visc_start, dens_start, slot_live = inputs
        return marker_blocks(received, places, visc_start, dens_start, slot_live)

    marker_visc, moments = lax.map(
        owner_work, (fetched, positions, start_visc, marker_dens, live_slots)
    )
    catalog = jnp.arange(bricks.shape[0], dtype=jnp.int32)
    one_hot = (block_brick[:, :, None] == catalog).astype(jnp.float32)
    per_owner = jnp.einsum("psb,psq->pbq", one_hot, moments, precision=highest)
    moment_sums = lax.psum_scatter(per_owner, "mark", scatter_dimension=0, tiled=True)[0]
    cell_moments = (
        moment_sums.reshape(size_x // 4, size_y // 4, size_z // 8, 3, 4, 4, 8)
        .transpose(3, 0, 4, 1, 5, 2, 6)
        .reshape(3, size_x, size_y, size_z)
    )
    visc_next = jnp.exp((cell_moments[1] + jnp.log(cell_visc)) / (cell_moments[0] + 1.0))
    dens_next = (cell_moments[2] + cell_dens) / (cell_moments[0] + 1.0)
    return (unknowns[:3], unknowns[3], visc_next, dens_next, marker_visc)


def solution(mesh):
    in_specs = (
        P(None, "grid", "mark", None),
        P("grid", "mark", None),
        P("grid", "mark", None),
        P("grid", "mark", None),
        P(("grid", "mark"), None),
        P(("grid", "mark"), None),
        P(("grid", "mark"), None, None, None),
        P(("grid", "mark"), None, None),
        P(("grid", "mark"), None, None),
    )
    out_specs = (
        P(None, "grid", "mark", None),
        P("grid", "mark", None),
        P("grid", "mark", None),
        P("grid", "mark", None),
        P(("grid", "mark"), None, None),
    )
    return jax.shard_map(
        per_device, mesh=mesh, in_specs=in_specs, out_specs=out_specs, check_vma=False
    )
```

profile of v0, /device:TPU:38, one launch (start us, length us, event | category | flops | bytes accessed | tf_op | source)
XLA Modules:
  0.0 1040.2 jit_solution(8659642746502254343)
XLA Ops:
  7.2 17.1 %reshape.311 = f32[3,8,4,4,4,32,8]{6,5,4,3,2,1,0:T(8,128)} reshape(f32[3,32,16,256]{3,2,1,0:T(8,128)} %param.11) | data formatting | bytes 3145728 | tf_op jit(solution)/shard_map/reshape | solution.py:131
  24.4 16.7 %copy.52 = f32[8,4,32,3,4,4,8]{2,1,0,6,5,4,3:T(4,128)} copy(f32[8,4,32,3,4,4,8]{6,2,5,1,4,0,3:T(8,128)} %bitcast.128) | data formatting | bytes 3145728 | tf_op jit(solution)/shard_map/transpose | solution.py:132
  41.1 7.5 reshape.312
  51.1 155.3 %all-gather.2.cloned.1.call-done = f32[16384,384]{1,0:T(8,128)} async-done(((f32[1024,384]{1,0:T(8,128)}), f32[16384,384]{1,0:T(8,128)}) %all-gather.2.cloned.1.call-update) | async-done | bytes 25165840 | tf_op jit(solution)/shard_map/all_gather | solution.py:136
  206.5 11.4 %gather_fusion = f32[768,384]{1,0:T(8,128)} fusion(f32[16384,384]{1,0:T(8,128)} %all-gather.2.cloned.1.call-done, s32[1024]{0:T(1024)S(1)} %pad_clamp_fusion), kind=kCustom, calls=%fused_computation | custom fusion | bytes 2362368 | tf_op jit(solution)/shard_map/gather | solution.py:138
  217.8 513.2 %while.12 = (s32[]{:T(128)}, f32[16,48,256]{2,1,0:T(8,128)}, f32[16,48,384]{1,2,0:T(8,128)}, pred[16,48]{1,0:T(8,128)(4,1)}, f32[16,48,256]{2,1,0:T(8,128)}, /*i...) while((s32[]{:T(128)}, f32[16,48,256]{2,1,0:T(8,128)}, ...), condition=%wide.region_10.11_spmd, body=%wide.region_0.10_spmd.sunk | while | flops 178716736 | bytes 41928088 | solution.py:147
  222.4 3.5 fusion.316
  230.4 3.1 multiply_reduce_fusion.5
  254.4 3.5 fusion.316
  262.4 3.1 multiply_reduce_fusion.5
  286.5 3.5 fusion.316
  294.4 3.1 multiply_reduce_fusion.5
  318.5 3.5 fusion.316
  326.5 3.1 multiply_reduce_fusion.5
  350.5 3.5 fusion.316
  358.5 3.1 multiply_reduce_fusion.5
  382.6 3.5 fusion.316
  390.5 3.1 multiply_reduce_fusion.5
  414.6 3.5 fusion.316
  422.6 3.1 multiply_reduce_fusion.5
  446.6 3.5 fusion.316
  454.6 3.1 multiply_reduce_fusion.5
  478.7 3.5 fusion.316
  486.6 3.1 multiply_reduce_fusion.5
  510.7 3.5 fusion.316
  518.7 3.1 multiply_reduce_fusion.5
  542.7 3.5 fusion.316
  550.7 3.1 multiply_reduce_fusion.5
  574.8 3.5 fusion.316
  582.8 3.1 multiply_reduce_fusion.5
  606.8 3.5 fusion.316
  638.8 3.5 fusion.316
  646.8 3.1 multiply_reduce_fusion.5
  670.9 3.5 fusion.316
  702.9 3.5 fusion.316
  710.9 3.1 multiply_reduce_fusion.5
  731.0 17.9 %fusion.65 = f32[16,1024,384]{2,1,0:T(8,128)} fusion(f32[16,48,384]{1,2,0:T(8,128)} %get-tuple-element.48, s32[16,48]{1,0:T(8,128)S(1)} %copy-done.13), kind=kOutput, calls=%fused_computation.127 | convolution fusion | flops 3625451520 | bytes 26348544 | tf_op jit(solution)/shard_map/psb,psq->pbq/dot_general | solution.py:152
  755.0 3.4 collective-permute-done
  758.6 4.7 collective-permute-start.3
  767.3 3.6 collective-permute-start.4
  770.9 4.8 collective-permute-done.2
  775.7 5.1 select_maximum_fusion
  784.3 3.9 collective-permute-start.7
  789.1 3.9 collective-permute-done.7
  802.0 3.2 collective-permute-done.8
  807.3 4.1 collective-permute-start.10
  811.5 4.6 collective-permute-done.11
  816.1 4.0 collective-permute-done.10
  828.8 79.8 %reduce-scatter.4.cloned.1.call-done = f32[1,1024,384]{2,1,0:T(8,128)} async-done(((f32[16,1024,384]{2,1,0:T(8,128)}), f32[1,1024,384]{2,1,0:T(8,128)}) %reduce-scatter.4.cloned.1.call-update) | async-done | bytes 1572880
  911.6 6.1 reshape_squeeze.3
  917.7 6.4 copy.82
  927.0 6.5 copy.61
  933.6 7.7 add.574
  941.2 6.4 copy.62
  947.6 7.7 squeeze.98
  955.2 6.4 copy.60
  961.6 7.7 squeeze.97
  969.2 6.1 add_divide_fusion
  979.7 3.5 collective-permute-done.12
  983.4 4.8 collective-permute-start.15
  990.8 6.5 collective-permute-done.14
  1009.0 3.2 collective-permute-done.16
  1014.3 3.9 collective-permute-start.18
  1019.3 4.0 collective-permute-done.18
  (678 shorter events, 484.9 us)
Async XLA Ops:
  7.2 199.3 %all-gather.2.cloned.1.call-start = ((), (), s32[]{:S(2)}) async-start(), calls=%async_computation.1 | async-start | bytes 26738688 | tf_op jit(solution)/shard_map/all_gather | solution.py:136
  50.2 858.4 %reduce-scatter.4.cloned.1.call-start = ((), (), s32[]{:S(2)}) async-start(), calls=%async_computation.2 | async-start | bytes 26738688
  237.6 2.9 copy-start.6
  237.6 2.9 copy-start.7
  237.6 3.5 copy-start.14
  269.7 2.9 copy-start.6
  269.7 2.9 copy-start.7
  269.7 3.5 copy-start.14
  301.7 2.9 copy-start.7
  301.7 3.5 copy-start.14
  333.8 2.9 copy-start.7
  333.8 3.5 copy-start.14
  365.8 2.9 copy-start.7
  365.8 3.5 copy-start.14
  397.8 2.9 copy-start.6
  397.8 2.9 copy-start.7
  397.8 3.5 copy-start.14
  429.9 2.9 copy-start.7
  429.9 3.5 copy-start.14
  461.9 2.9 copy-start.7
  461.9 3.5 copy-start.14
  493.9 2.9 copy-start.7
  493.9 3.5 copy-start.14
  526.0 2.9 copy-start.7
  526.0 3.5 copy-start.14
  558.0 2.9 copy-start.7
  558.0 3.5 copy-start.14
  590.0 2.9 copy-start.7
  590.0 3.5 copy-start.14
  622.1 2.9 copy-start.7
  622.1 3.5 copy-start.14
  654.1 2.9 copy-start.6
  654.1 2.9 copy-start.7
  654.1 3.5 copy-start.14
  686.1 2.9 copy-start.7
  686.1 3.5 copy-start.14
  718.2 2.9 copy-start.7
  718.2 3.5 copy-start.14
  750.5 14.8 %copy-start = (f32[32,16,256]{2,1,0:T(8,128)S(1)}, f32[32,16,256]{2,1,0:T(8,128)}, u32[]{:S(2)}) copy-start(f32[32,16,256]{2,1,0:T(8,128)} %param.13) | copy-start | bytes 1572868
  750.5 4.5 collective-permute-start.1
  752.9 5.6 collective-permute-start
  758.6 12.3 %collective-permute-start.3 = (f32[4,34,1,256]{3,2,1,0:T(1,128)S(1)}, f32[4,34,1,256]{3,2,1,0:T(1,128)S(1)}, u32[]{:S(2)}, u32[]{:S(2)}) collective-permute-start(f32[4,34,1,256]{3,2,1,0:T(1,128)S(1)} %get-tuple-element.171), channel_id=1, source_target_pairs={{1,0},{2,1},{3,2},{4,3},{5,4},{6,5},{7,6},{8,7},{9,8},{10,9},{11,1... | collective-permute-start | bytes 417800 | tf_op jit(solution)/shard_map/ppermute | solution.py:23
  763.4 12.3 %collective-permute-start.2 = (f32[4,34,1,256]{3,2,1,0:T(1,128)S(1)}, f32[4,34,1,256]{3,2,1,0:T(1,128)S(1)}, u32[]{:S(2)}, u32[]{:S(2)}) collective-permute-start(f32[4,34,1,256]{3,2,1,0:T(1,128)S(1)} %get-tuple-element.170), channel_id=1, source_target_pairs={{0,1},{1,2},{2,3},{3,4},{4,5},{5,6},{6,7},{7,8},{8,9},{9,10},{10,1... | collective-permute-start | bytes 417800 | tf_op jit(solution)/shard_map/ppermute | solution.py:22
  765.3 5.6 collective-permute-start.5
  767.3 15.0 %collective-permute-start.4 = (f32[1,16,256]{2,1,0:T(8,128)S(1)}, f32[1,16,256]{2,1,0:T(8,128)S(1)}, u32[]{:S(2)}, u32[]{:S(2)}) collective-permute-start(f32[1,16,256]{2,1,0:T(8,128)S(1)} %get-tuple-element.188), channel_id=1, source_target_pairs={{16,0},{32,16},{48,32},{64,48},{80,64},{96,80},{112,96},{17,1},{33... | collective-permute-start | bytes 49160 | tf_op jit(solution)/shard_map/ppermute | solution.py:23
  782.3 6.7 collective-permute-start.6
  784.3 8.7 collective-permute-start.7
  797.7 4.3 collective-permute-start.9
  799.6 5.6 collective-permute-start.8
  805.4 10.6 %collective-permute-start.11 = (f32[4,34,1,256]{3,2,1,0:T(1,128)S(1)}, f32[4,34,1,256]{3,2,1,0:T(1,128)S(1)}, u32[]{:S(2)}, u32[]{:S(2)}) collective-permute-start(f32[4,34,1,256]{3,2,1,0:T(1,128)S(1)} %get-tuple-element.169), channel_id=1, source_target_pairs={{1,0},{2,1},{3,2},{4,3},{5,4},{6,5},{7,6},{8,7},{9,8},{10,9},{11,1... | collective-permute-start | bytes 417800 | tf_op jit(solution)/shard_map/ppermute | solution.py:23
  807.3 12.7 %collective-permute-start.10 = (f32[4,34,1,256]{3,2,1,0:T(1,128)S(1)}, f32[4,34,1,256]{3,2,1,0:T(1,128)S(1)}, u32[]{:S(2)}, u32[]{:S(2)}) collective-permute-start(f32[4,34,1,256]{3,2,1,0:T(1,128)S(1)} %get-tuple-element.168), channel_id=1, source_target_pairs={{0,1},{1,2},{2,3},{3,4},{4,5},{5,6},{6,7},{7,8},{8,9},{9,10},{10,1... | collective-permute-start | bytes 417800 | tf_op jit(solution)/shard_map/ppermute | solution.py:22
  822.4 4.5 copy-start.3
  822.4 4.5 copy-start.5
  969.2 6.1 copy-start.9
  969.2 6.1 copy-start.10
  969.2 6.1 copy-start.11
  975.4 4.3 collective-permute-start.13
  977.6 5.6 collective-permute-start.12
  983.4 7.3 collective-permute-start.15
  988.2 9.1 collective-permute-start.14
  1004.7 4.3 collective-permute-start.17
  1006.6 5.6 collective-permute-start.16
  1012.4 6.9 collective-permute-start.19
  1014.3 9.1 collective-permute-start.18
  (19 other events, 47.4 us)
Sparse Core Ops, SparseCore 0:
  50.3 156.0 all-gather.1
  749.1 159.4 reduce-scatter.3
where the time goes:
time: 1050 us; the launch traced here: 1040 us
  local copies, waits for them, and re-layouts  289 us (28%)
  waiting for transfers between devices  279 us (27%)
  other arithmetic  258 us (25%)
  matrix products  142 us (14%)
  starting transfers between devices  54.1 us (5%)
  between operations  15.1 us (1%)
    all_gather x1, waiting for transfers between devices, per_device(): whole_slab = lax.all_gather(bricks, 'mark', axis=0, tiled=True)  155 us
    unnamed x3, waiting for transfers between devices  79.8 us
    dot_general x16, matrix products, marker_blocks(): jnp.einsum('kcz,kzm->kcm', values, across_z, precision=highest)  55.9 us
    reduce_sum x16, other arithmetic, marker_blocks(): grad_x = jnp.sum(interpolated * plane_dx[:, None], axis=(2, 3))  49.7 us
    reduce_sum x16, other arithmetic, marker_blocks(): grad_z = jnp.sum(rising * plane_xy[:, None], axis=(2, 3))  46.1 us
    mul x16, local copies, waits for them, and re-layouts, marker_blocks(): carried[:, :, None, None, :] * plane_xy[:, None]  42.6 us
    reshape x16, local copies, waits for them, and re-layouts, marker_blocks(): jnp.einsum('kcz,kzm->kcm', values, across_z, precision=highest)  41.7 us
    ppermute x10, waiting for transfers between devices, extended(): before = lax.ppermute(last, axis, up)  36.5 us
  transfers between devices with their start and end apart: 22, of which 15 were waited for; matrix products, arithmetic and copies ran while one was open for 2% of the time, Pallas kernels for 0%

commit v1 on v0

v1 whole, which is shorter than its diff:
```python
import functools
import math
import jax
import jax.numpy as jnp
from jax import lax
from jax.sharding import PartitionSpec as P
from jax.experimental import pallas as pl
from jax.experimental.pallas import tpu as pltpu

F32, BF16 = jnp.float32, jnp.bfloat16
VMEM = pltpu.VMEM
CAP, BLOCK, OWNERS = 48, 256, 16
NT = (((1,), (1,)), ((), ()))
UNROLL = 4


def split(x):
    hi = x.astype(BF16)
    return hi, (x - hi.astype(F32)).astype(BF16)


def axis_weights(fraction, cells):
    half = 0.5 * cells
    factor = jnp.exp(2.0 * cells * fraction - 2.0 * half)
    centres = [i + 0.5 - half for i in range(cells)]
    powers = [None, factor]
    for i in range(2, cells):
        powers.append(powers[i // 2] * powers[i - i // 2])
    raw = [jnp.full_like(factor, math.exp(-centres[0] ** 2))]
    raw += [math.exp(-(centres[i] ** 2)) * powers[i] for i in range(1, cells)]
    total = functools.reduce(jnp.add, raw)
    scale = 1.0 / total
    weights = [r * scale for r in raw]
    mean = functools.reduce(jnp.add, [c * w for c, w in zip(centres, weights)])
    return weights, mean


def marker_group(q, row, u, pos, visc, dens, bricks, marker_out, moments, count, wz_s, wy_s, planes):
    rows = pl.ds(row, 8)
    sub = lax.broadcasted_iota(jnp.int32, (8, 128), 0)
    lane = lax.broadcasted_iota(jnp.int32, (8, 128), 1)
    sub2 = lax.broadcasted_iota(jnp.int32, (8, 256), 0)
    low, low2 = sub < 4, sub2 < 4
    diag = (lane // 32) == (sub % 4)
    shifts = [(sub - (2 * ip + sub // 4) + 4) % 4 for ip in range(2)]
    spread = [[diag & (shifts[ip] == s) for s in range(4)] for ip in range(2)]

    def both(x):
        wide = x.shape[1] == 256
        turned = pltpu.roll(x, 4, 0)
        mask = low2 if wide else low
        return jnp.where(mask, x, turned), jnp.where(mask, turned, x)

    wx, mean_x = axis_weights(pos[q, 0, rows, :], 4)
    wy, mean_y = axis_weights(pos[q, 1, rows, :], 4)
    wz, mean_z = axis_weights(pos[q, 2, rows, :], 8)
    for k in range(8):
        for h in range(2):
            wz_s[u, h, pl.ds(8 * k, 8), :] = wz[k][:, 128 * h : 128 * h + 128]
    for j in range(4):
        for h in range(2):
            wy_s[u, h, pl.ds(8 * j, 8), :] = wy[j][:, 128 * h : 128 * h + 128]
    for b in range(8):
        for h in range(2):
            col = wz_s[u, h, pl.ds(b, 8, stride=8), :]
            for jp in range(2):
                pair = [
                    col * jnp.broadcast_to(wy_s[u, h, pl.ds(8 * j + b, 1), :], (8, 128))
                    for j in (2 * jp, 2 * jp + 1)
                ]
                hi, lo = split(jnp.concatenate(pair, axis=0))
                at = 32 * (b % 4) + 16 * jp
                planes[u, b // 4, pl.ds(at, 16), pl.ds(128 * h, 128)] = hi
                planes[u, b // 4, pl.ds(128 + at, 16), pl.ds(128 * h, 128)] = lo

    cell = lane.astype(F32)
    c_i = (lane // 32).astype(F32) - 1.5
    c_j = ((lane // 8) % 4).astype(F32) - 1.5
    c_k = (lane % 8).astype(F32) - 3.5
    v = [bricks[q, rows, pl.ds(128 * c, 128)] for c in range(3)]
    kinds = [
        v[0],
        v[1],
        v[2],
        c_j * v[1],
        c_k * v[2],
        c_j * v[0] + c_i * v[1],
        c_k * v[0] + c_i * v[2],
        c_k * v[1] + c_j * v[2],
    ]
    tiles = ([], [])
    for kind in kinds:
        for side, src in enumerate(both(kind)):
            turned = [src] + [pltpu.roll(src, 32 * s, 1) for s in range(1, 4)]
            for ip in range(2):
                tile = jnp.zeros_like(src)
                for s in range(4):
                    tile = jnp.where(spread[ip][s], turned[s], tile)
                tiles[side].append(tile)
    results = []
    for side in range(2):
        his, los = [], []
        for n in range(0, 16, 2):
            hi, lo = split(jnp.concatenate(tiles[side][n : n + 2], axis=0))
            his.append(hi)
            los.append(lo)
        left = jnp.concatenate(his + los, axis=0)
        left = jnp.concatenate([left, left], axis=1)
        out = jnp.dot(left, planes[u, side], preferred_element_type=F32)
        results.append(out[:128] + out[128:])
    pairs = ([], [])
    centred = ([], [])
    for ip in range(2):
        first, second = both(wx[2 * ip]), both(wx[2 * ip + 1])
        for side in range(2):
            w = jnp.where(low2, first[side], second[side])
            c = jnp.where(low2, 2 * ip - 1.5, 2 * ip - 0.5)
            pairs[side].append(w)
            centred[side].append(w * c)

    def fold(a, b):
        return jnp.where(low2, a, b) + pltpu.roll(jnp.where(low2, b, a), 4, 0)

    def along_x(kind, weights):
        sums = []
        for side in range(2):
            at = 16 * kind
            sums.append(
                results[side][at : at + 8] * weights[side][0]
                + results[side][at + 8 : at + 16] * weights[side][1]
            )
        return fold(*sums)

    vx, vy, vz, yy, zz, xy, xz, yz = [along_x(n, pairs) for n in range(8)]
    xx = along_x(0, centred) - mean_x * vx
    yy = yy - mean_y * vy
    zz = zz - mean_z * vz
    xy = xy - mean_y * vx - mean_x * vy
    xz = xz - mean_z * vx - mean_x * vz
    yz = yz - mean_z * vy - mean_y * vz
    invariant = 2.0 * (xx * xx + yy * yy + zz * zz) + xy * xy + xz * xz + yz * yz
    shift = jnp.log(1.0 + invariant * 4.0) * (1.0 / 3.0)
    start = visc[q, rows, :]
    live = (sub2 + row) < count
    weakened = start * jnp.exp(-shift)
    marker_out[q, rows, :] = jnp.where(live, weakened, 0.0)
    carried = [
        jnp.where(live, 1.0, 0.0),
        jnp.where(live, jnp.log(weakened), 0.0),
        jnp.where(live, dens[q, rows, :], 0.0),
    ]
    carried = [both(c) for c in carried]
    sums = []
    for side in range(2):
        rows_a = [carried[m][side] * pairs[side][ip] for m in range(3) for ip in range(2)]
        his, los = [], []
        for n in range(0, 6, 2):
            hi, lo = split(jnp.concatenate(rows_a[n : n + 2], axis=0))
            his.append(hi)
            los.append(lo)
        left = jnp.concatenate(his + los, axis=0)
        out = lax.dot_general(left, planes[u, side], NT, preferred_element_type=F32)
        sums.append(out[:48, :128] + out[:48, 128:] + out[48:, :128])
    for m in range(3):
        halves = []
        for side in range(2):
            total = None
            for ip in range(2):
                at = 16 * m + 8 * ip
                piece = jnp.where(diag, sums[side][at : at + 8], 0.0)
                placed = piece
                for s in range(1, 4):
                    placed = jnp.where(shifts[ip] == (4 - s), pltpu.roll(piece, 32 * s, 1), placed)
                total = placed if total is None else total + placed
            halves.append(total)
        moments[q, rows, pl.ds(128 * m, 128)] = jnp.where(low, halves[0], halves[1]) + pltpu.roll(
            jnp.where(low, halves[1], halves[0]), 4, 0
        )


def marker_kernel(counts, pos, visc, dens, bricks, marker_out, moments, todo, wz_s, wy_s, planes):
    def clear(q, _):
        marker_out[q] = jnp.zeros((CAP, BLOCK), F32)
        moments[q] = jnp.zeros((CAP, 384), F32)
        return 0

    lax.fori_loop(0, OWNERS, clear, 0)

    def listed(q, n):
        groups = (counts[0, q] + 7) // 8

        def put(g, at):
            todo[at] = q * 8 + g
            return at + 1

        return lax.fori_loop(0, groups, put, n)

    total = lax.fori_loop(0, OWNERS, listed, 0)

    def step(n, _):
        for u in range(UNROLL):
            item = todo[jnp.minimum(n * UNROLL + u, total - 1)]
            q = item // 8
            row = pl.multiple_of((item % 8) * 8, 8)
            marker_group(
                q, row, u, pos, visc, dens, bricks, marker_out, moments, counts[0, q], wz_s, wy_s, planes
            )
        return 0

    lax.fori_loop(0, (total + UNROLL - 1) // UNROLL, step, 0)


def marker_call(counts, pos, visc, dens, bricks):
    vm = pl.BlockSpec(memory_space=pltpu.VMEM)
    return pl.pallas_call(
        marker_kernel,
        out_shape=(
            jax.ShapeDtypeStruct((OWNERS, CAP, BLOCK), F32),
            jax.ShapeDtypeStruct((OWNERS, CAP, 384), F32),
        ),
        in_specs=[pl.BlockSpec(memory_space=pltpu.SMEM)] + [vm] * 4,
        out_specs=(vm, vm),
        scratch_shapes=[
            pltpu.SMEM((OWNERS * 8 + 8,), jnp.int32),
            VMEM((UNROLL, 2, 64, 128), F32),
            VMEM((UNROLL, 2, 32, 128), F32),
            VMEM((UNROLL, 2, 256, 256), BF16),
        ],
        compiler_params=pltpu.CompilerParams(vmem_limit_bytes=50 << 20),
        name="markers",
    )(counts, pos, visc, dens, bricks)


NX_L, NY_L, NZ = 32, 16, 256
BRICKS = 1024
MESH = pl.DeviceIdType.MESH
SWEEPS = 4
relax_weight = 0.6
pressure_rate = 0.25
gravity = 1.0


def group_transpose(tiles, group):
    tiles = list(tiles)
    for d in (8, 4, 2, 1):
        upper = (group & d) != 0
        for t in range(16):
            if t & d == 0:
                a, b = tiles[t], tiles[t + d]
                tiles[t] = jnp.where(upper, pltpu.roll(b, 8 * d, 1), a)
                tiles[t + d] = jnp.where(upper, b, pltpu.roll(a, 128 - 8 * d, 1))
    return tiles


def peers():
    g, me = lax.axis_index("grid"), lax.axis_index("mark")

    def after(k):
        return lax.rem(me + k, OWNERS)

    def before(k):
        return lax.rem(me + OWNERS - k, OWNERS)

    return g, me, after, before


def remote(src, dst, send, recv, device):
    return pltpu.make_async_remote_copy(
        src_ref=src, dst_ref=dst, send_sem=send, recv_sem=recv, device_id=device, device_id_type=MESH
    )


def grid_kernel(
    brick_ids, velocity, pressure, visc, dens, ids_out, bricks_out, velocity_out, pressure_out,
    state_a, state_b, visc_s, dens_s, halves, planes_hi, planes_lo, one_hot, ids_send, ids_recv, brick_send,
    kx, kym, kyp, kzm, kzp, damp, x_lo, x_hi, face_lo, face_hi, y_lo, y_hi,
    vx_lo, vx_hi, vface_lo, vface_hi, vy_lo, vy_hi,
    load_sem, id_send, id_recv, b_send, b_recv, h_send, h_recv, v_send, v_recv,
):
    g, me, after, before = peers()
    ahead, behind = lax.rem(g + 1, 8), lax.rem(g + 7, 8)
    loads = [
        pltpu.make_async_copy(velocity, state_a.at[pl.ds(0, 3), pl.ds(1, NX_L)], load_sem.at[0]),
        pltpu.make_async_copy(pressure, state_a.at[3, pl.ds(1, NX_L)], load_sem.at[1]),
        pltpu.make_async_copy(visc, visc_s.at[pl.ds(1, NX_L)], load_sem.at[2]),
        pltpu.make_async_copy(dens, dens_s, load_sem.at[3]),
    ]
    for c in loads:
        c.start()
    barrier = pltpu.get_barrier_semaphore()
    for k in range(1, OWNERS):
        pl.semaphore_signal(barrier, inc=1, device_id=(g, after(k)), device_id_type=MESH)
    pl.semaphore_signal(barrier, inc=1, device_id=(ahead, me), device_id_type=MESH)
    pl.semaphore_signal(barrier, inc=1, device_id=(behind, me), device_id_type=MESH)

    number = brick_ids[...]
    number = (((number >> 5) & 3) * 32 + (number & 31)) * 8 + (number >> 7)
    number = number.astype(F32)
    ids_send[...] = jnp.full((OWNERS, 8, 128), -1.0, F32)
    for q in range(OWNERS):
        ids_send[q, :, pl.ds(0, CAP)] = jnp.broadcast_to(number[q : q + 1], (8, CAP))
    pl.semaphore_wait(barrier, OWNERS + 1)

    def send_ids(k, _):
        remote(ids_send.at[after(k)], ids_recv.at[k], id_send.at[k], id_recv.at[k], (g, after(k))).start()
        return 0

    lax.fori_loop(1, OWNERS, send_ids, 0)
    ids_recv[0] = ids_send[me]
    for c in loads:
        c.wait()

    def halo(n, state):
        return [
            remote(state.at[:, 1], x_hi.at[n], h_send.at[n, 0], h_recv.at[n, 0], (behind, me)),
            remote(state.at[:, NX_L], x_lo.at[n], h_send.at[n, 1], h_recv.at[n, 1], (ahead, me)),
            remote(face_lo.at[n], y_hi.at[n], h_send.at[n, 2], h_recv.at[n, 2], (g, before(1))),
            remote(face_hi.at[n], y_lo.at[n], h_send.at[n, 3], h_recv.at[n, 3], (g, after(1))),
        ]

    def first_faces(x, _):
        face_lo[0, x] = jnp.concatenate([state_a[c, x + 1, 0:1, :] for c in range(4)], axis=0)
        face_hi[0, x] = jnp.concatenate([state_a[c, x + 1, 15:16, :] for c in range(4)], axis=0)
        return 0

    lax.fori_loop(0, NX_L, first_faces, 0)
    for x in range(NX_L):
        vface_lo[x : x + 1, :] = visc_s[x + 1, 0:1, :]
        vface_hi[x : x + 1, :] = visc_s[x + 1, 15:16, :]
    visc_halo = [
        remote(visc_s.at[1], vx_hi, v_send.at[0], v_recv.at[0], (behind, me)),
        remote(visc_s.at[NX_L], vx_lo, v_send.at[1], v_recv.at[1], (ahead, me)),
        remote(vface_lo, vy_hi, v_send.at[2], v_recv.at[2], (g, before(1))),
        remote(vface_hi, vy_lo, v_send.at[3], v_recv.at[3], (g, after(1))),
    ]
    for c in halo(0, state_a) + visc_halo:
        c.start()

    def to_halves(x, _):
        for c in range(3):
            plane = state_a[c, x + 1]
            at = pl.multiple_of(c * 512 + x * 16, 16)
            for h in range(2):
                halves[h, pl.ds(at, 16), :] = plane[:, 128 * h : 128 * h + 128]
        return 0

    lax.fori_loop(0, NX_L, to_halves, 0)
    group = lax.broadcasted_iota(jnp.int32, (8, 128), 1) // 8

    def to_bricks(n, _):
        bj, h = n // 2, lax.rem(n, 2)
        for c in range(3):
            tiles = [
                halves[h, pl.ds(c * 512 + 16 * i + 4 * bj + j, 8, stride=64), :]
                for i in range(4)
                for j in range(4)
            ]
            tiles = group_transpose(tiles, group)
            for t in range(0, 16, 2):
                hi, lo = split(jnp.concatenate(tiles[t : t + 2], axis=0))
                at = pl.multiple_of((bj * 32 + h * 16 + t) * 8, 16)
                planes_hi[pl.ds(at, 16), pl.ds(128 * c, 128)] = hi
                planes_lo[pl.ds(at, 16), pl.ds(128 * c, 128)] = lo
        return 0

    lax.fori_loop(0, 8, to_bricks, 0)

    def wait_ids(k, _):
        remote(ids_send.at[after(k)], ids_recv.at[k], id_send.at[k], id_recv.at[k], (g, after(k))).wait()
        return 0

    lax.fori_loop(1, OWNERS, wait_ids, 0)

    def brick_copy(k):
        return remote(
            brick_send.at[k], bricks_out.at[me], b_send.at[k], b_recv.at[k], (g, before(k))
        )

    lanes = lax.broadcasted_iota(jnp.int32, (CAP, 128), 1).astype(F32)

    def gather(n, _):
        for m in range(4):
            column = jnp.transpose(jnp.broadcast_to(ids_recv[4 * n + m][0:1, :], (128, 128)))[:CAP]
            for t in range(8):
                hit = jnp.where(column == lanes + 128.0 * t, 1.0, 0.0).astype(BF16)
                one_hot[pl.ds(CAP * m, CAP), pl.ds(128 * t, 128)] = hit
        found = jnp.dot(one_hot[...], planes_hi[...], preferred_element_type=F32)
        found = found + jnp.dot(one_hot[...], planes_lo[...], preferred_element_type=F32)
        for m in range(4):
            brick_send[4 * n + m] = found[CAP * m : CAP * m + CAP]
        for m in range(4):
            k = 4 * n + m

            @pl.when(k > 0)
            def _():
                brick_copy(k).start()

        return 0

    lax.fori_loop(0, 4, gather, 0)
    own = pltpu.make_async_copy(brick_send.at[0], bricks_out.at[me], load_sem.at[4])
    own.start()
    ids_out[...] = ids_recv[...]

    x_lo_on = (g > 0).astype(F32)
    x_hi_on = (g < 7).astype(F32)
    y_lo_on = (me > 0).astype(F32)
    y_hi_on = (me < OWNERS - 1).astype(F32)
    row = lax.broadcasted_iota(jnp.int32, (NY_L, NZ), 0)
    col = lax.broadcasted_iota(jnp.int32, (NY_L, NZ), 1)
    first_y, last_y = row == 0, row == NY_L - 1
    first_z, last_z = col == 0, col == NZ - 1

    def y_minus(plane, edge):
        return jnp.where(first_y, jnp.broadcast_to(edge, plane.shape), pltpu.roll(plane, 1, 0))

    def y_plus(plane, edge):
        return jnp.where(last_y, jnp.broadcast_to(edge, plane.shape), pltpu.roll(plane, NY_L - 1, 0))

    def z_minus(plane):
        return jnp.where(first_z, 0.0, pltpu.roll(plane, 1, 1))

    def z_plus(plane):
        return jnp.where(last_z, 0.0, pltpu.roll(plane, NZ - 1, 1))

    for c in visc_halo:
        c.wait()
    visc_s[0] = vx_lo[...] * x_lo_on
    visc_s[NX_L + 1] = vx_hi[...] * x_hi_on

    def couplings(x, _):
        here, below, above = visc_s[x + 1], visc_s[x], visc_s[x + 2]
        k_xm, k_xp = 0.5 * (here + below), 0.5 * (here + above)
        k_ym = 0.5 * (here + y_minus(here, vy_lo[pl.ds(x, 1), :] * y_lo_on))
        k_yp = 0.5 * (here + y_plus(here, vy_hi[pl.ds(x, 1), :] * y_hi_on))
        k_zm, k_zp = 0.5 * (here + z_minus(here)), 0.5 * (here + z_plus(here))
        kx[x] = k_xm
        kx[x + 1] = k_xp
        kym[x] = k_ym
        kyp[x] = k_yp
        kzm[x] = k_zm
        kzp[x] = k_zp
        damp[x] = relax_weight / (k_xm + k_xp + k_ym + k_yp + k_zm + k_zp)
        return 0

    lax.fori_loop(0, NX_L, couplings, 0)

    for n in range(SWEEPS):
        old, new = (state_a, state_b) if n % 2 == 0 else (state_b, state_a)
        for c in halo(n, old):
            c.wait()
        old[:, 0] = x_lo[n] * x_lo_on
        old[:, NX_L + 1] = x_hi[n] * x_hi_on

        def sweep(x, _, n=n, old=old, new=new):
            low = y_lo[n, x] * y_lo_on
            high = y_hi[n, x] * y_hi_on
            press = old[3, x + 1]
            press_near = [
                old[3, x],
                y_minus(press, low[3:4]),
                z_minus(press),
            ]
            weights = [kx[x + 1], kx[x], kyp[x], kym[x], kzp[x], kzm[x]]
            scale = damp[x]
            divergence = jnp.zeros_like(press)
            fresh = []
            for c in range(3):
                v = old[c, x + 1]
                near = [
                    old[c, x + 2],
                    old[c, x],
                    y_plus(v, high[c : c + 1]),
                    y_minus(v, low[c : c + 1]),
                    z_plus(v),
                    z_minus(v),
                ]
                forcing = press_near[c] - press
                for w, s in zip(weights, near):
                    forcing = forcing + w * (s - v)
                if c == 2:
                    forcing = forcing - gravity * dens_s[x]
                fresh.append(v + scale * forcing)
                divergence = divergence + (near[2 * c] - v)
            fresh.append(press - pressure_rate * visc_s[x + 1] * divergence)
            for c in range(4):
                new[c, x + 1] = fresh[c]
            if n + 1 < SWEEPS:
                face_lo[n + 1, x] = jnp.concatenate([f[0:1] for f in fresh], axis=0)
                face_hi[n + 1, x] = jnp.concatenate([f[15:16] for f in fresh], axis=0)
            return 0

        lax.fori_loop(0, NX_L, sweep, 0)
        if n + 1 < SWEEPS:
            for c in halo(n + 1, new):
                c.start()
    last = state_a if SWEEPS % 2 == 0 else state_b
    stores = [
        pltpu.make_async_copy(last.at[pl.ds(0, 3), pl.ds(1, NX_L)], velocity_out, load_sem.at[5]),
        pltpu.make_async_copy(last.at[3, pl.ds(1, NX_L)], pressure_out, load_sem.at[6]),
    ]
    for c in stores:
        c.start()

    def wait_bricks(k, _):
        remote(
            brick_send.at[k], bricks_out.at[after(k)], b_send.at[k], b_recv.at[k], (g, before(k))
        ).wait()
        return 0

    lax.fori_loop(1, OWNERS, wait_bricks, 0)
    own.wait()
    for c in stores:
        c.wait()


def grid_call(block_brick, velocity, pressure, visc, dens):
    vm = pl.BlockSpec(memory_space=pltpu.VMEM)
    hbm = pl.BlockSpec(memory_space=pl.ANY)
    dma = pltpu.SemaphoreType.DMA
    field = (NX_L, NY_L, NZ)
    padded = (NX_L + 2, NY_L, NZ)
    return pl.pallas_call(
        grid_kernel,
        out_shape=(
            jax.ShapeDtypeStruct((OWNERS, 8, 128), F32),
            jax.ShapeDtypeStruct((OWNERS, CAP, 384), F32),
            jax.ShapeDtypeStruct((3,) + field, F32),
            jax.ShapeDtypeStruct(field, F32),
        ),
        in_specs=[vm] + [hbm] * 4,
        out_specs=(vm, hbm, hbm, hbm),
        scratch_shapes=[
            VMEM((4,) + padded, F32),
            VMEM((4,) + padded, F32),
            VMEM(padded, F32),
            VMEM(field, F32),
            VMEM((2, 1536, 128), F32),
            VMEM((BRICKS, 384), BF16),
            VMEM((BRICKS, 384), BF16),
            VMEM((4 * CAP, BRICKS), BF16),
            VMEM((OWNERS, 8, 128), F32),
            VMEM((OWNERS, 8, 128), F32),
            VMEM((OWNERS, CAP, 384), F32),
            VMEM((NX_L + 1, NY_L, NZ), F32),
            VMEM(field, F32),
            VMEM(field, F32),
            VMEM(field, F32),
            VMEM(field, F32),
            VMEM(field, F32),
            VMEM((SWEEPS, 4, NY_L, NZ), F32),
            VMEM((SWEEPS, 4, NY_L, NZ), F32),
            VMEM((SWEEPS, NX_L, 4, NZ), F32),
            VMEM((SWEEPS, NX_L, 4, NZ), F32),
            VMEM((SWEEPS, NX_L, 4, NZ), F32),
            VMEM((SWEEPS, NX_L, 4, NZ), F32),
            VMEM((NY_L, NZ), F32),
            VMEM((NY_L, NZ), F32),
            VMEM((NX_L, NZ), F32),
            VMEM((NX_L, NZ), F32),
            VMEM((NX_L, NZ), F32),
            VMEM((NX_L, NZ), F32),
            dma((7,)),
            dma((OWNERS,)),
            dma((OWNERS,)),
            dma((OWNERS,)),
            dma((OWNERS,)),
            dma((SWEEPS, 4)),
            dma((SWEEPS, 4)),
            dma((4,)),
            dma((4,)),
        ],
        compiler_params=pltpu.CompilerParams(
            collective_id=0, has_side_effects=True, vmem_limit_bytes=50 << 20
        ),
        name="grid_step",
    )(block_brick, velocity, pressure, visc, dens)


def moments_kernel(
    moments, ids, visc, dens, visc_out, dens_out,
    arrived, hits, hi_s, lo_s, sums, cells, send, recv, own_sem,
):
    g, me, after, before = peers()
    barrier = pltpu.get_barrier_semaphore()
    for k in range(1, OWNERS):
        pl.semaphore_signal(barrier, inc=1, device_id=(g, after(k)), device_id_type=MESH)
    pl.semaphore_wait(barrier, OWNERS - 1)

    def copy(k):
        return remote(moments.at[after(k)], arrived.at[k], send.at[k], recv.at[k], (g, after(k)))

    def start(k, _):
        copy(k).start()
        return 0

    lax.fori_loop(1, OWNERS, start, 0)
    own = pltpu.make_async_copy(moments.at[me], arrived.at[0], own_sem)
    own.start()

    lane = lax.broadcasted_iota(jnp.int32, (8, 128), 1)
    rows = [jnp.full((8, 128), -1.0, F32) for _ in range(6)]
    for k in range(OWNERS):
        at = CAP * k
        t, off = at // 128, at % 128
        tile = ids[k]
        turned = pltpu.roll(tile, off, 1) if off else tile
        rows[t] = jnp.where((lane >= off) & (lane < off + CAP), turned, rows[t])
        over = off + CAP - 128
        if over > 0:
            rows[t + 1] = jnp.where(lane < over, turned, rows[t + 1])

    wide = [jnp.concatenate([r, r], axis=0) for r in rows]
    sub = lax.broadcasted_iota(jnp.int32, (16, 128), 0).astype(F32)

    def mark_hits(r, _):
        at = pl.multiple_of(r * 16, 16)
        here = sub + (r * 16).astype(F32)
        for t in range(6):
            hits[pl.ds(at, 16), pl.ds(128 * t, 128)] = jnp.where(wide[t] == here, 1.0, 0.0).astype(BF16)
        return 0

    lax.fori_loop(0, BRICKS // 16, mark_hits, 0)

    def arrive(k, _):
        copy(k).wait()
        return 0

    own.wait()
    lax.fori_loop(1, OWNERS, arrive, 0)

    def pieces(k, _):
        hi, lo = split(arrived[k])
        at = pl.multiple_of(k * CAP, 16)
        hi_s[pl.ds(at, CAP), :] = hi
        lo_s[pl.ds(at, CAP), :] = lo
        return 0

    lax.fori_loop(0, OWNERS, pieces, 0)

    def scatter(n, _):
        at = pl.ds(pl.multiple_of(n * 256, 256), 256)
        block = hits[at, :]
        total = jnp.dot(block, hi_s[...], preferred_element_type=F32)
        total = total + jnp.dot(block, lo_s[...], preferred_element_type=F32)
        for m in range(3):
            sums[m, at, :] = total[:, 128 * m : 128 * m + 128]
        return 0

    lax.fori_loop(0, 4, scatter, 0)
    group = lane // 8

    def to_cells(n, _):
        bj, h = n // 2, lax.rem(n, 2)
        for m in range(3):
            tiles = [
                sums[m, pl.ds(pl.multiple_of((bj * 32 + h * 16 + t) * 8, 8), 8), :] for t in range(16)
            ]
            tiles = group_transpose(tiles, group)
            for i in range(4):
                for j in range(4):
                    cells[m, h, pl.ds(16 * i + 4 * bj + j, 8, stride=64), :] = tiles[4 * i + j]
        return 0

    lax.fori_loop(0, 8, to_cells, 0)

    def finish(x, _):
        at = pl.ds(pl.multiple_of(x * 16, 16), 16)
        for h in range(2):
            part = pl.ds(128 * h, 128)
            below = 1.0 / (cells[0, h, at, :] + 1.0)
            visc_out[x, :, part] = jnp.exp((cells[1, h, at, :] + jnp.log(visc[x, :, part])) * below)
            dens_out[x, :, part] = (cells[2, h, at, :] + dens[x, :, part]) * below
        return 0

    lax.fori_loop(0, NX_L, finish, 0)


def moments_call(moments, ids, visc, dens):
    vm = pl.BlockSpec(memory_space=pltpu.VMEM)
    hbm = pl.BlockSpec(memory_space=pl.ANY)
    dma = pltpu.SemaphoreType.DMA
    field = jax.ShapeDtypeStruct((NX_L, NY_L, NZ), F32)
    return pl.pallas_call(
        moments_kernel,
        out_shape=(field, field),
        in_specs=[hbm, vm, vm, vm],
        out_specs=(vm, vm),
        scratch_shapes=[
            VMEM((OWNERS, CAP, 384), F32),
            VMEM((BRICKS, OWNERS * CAP), BF16),
            VMEM((OWNERS * CAP, 384), BF16),
            VMEM((OWNERS * CAP, 384), BF16),
            VMEM((3, BRICKS, 128), F32),
            VMEM((3, 2, 512, 128), F32),
            dma((OWNERS,)),
            dma((OWNERS,)),
            dma,
        ],
        compiler_params=pltpu.CompilerParams(
            collective_id=1, has_side_effects=True, vmem_limit_bytes=50 << 20
        ),
        name="moments_home",
    )(moments, ids, visc, dens)


def per_device(
    velocity, pressure, cell_visc, cell_dens, block_brick, block_counts, positions, start_visc, marker_dens
):
    ids, bricks, velocity_next, pressure_next = grid_call(
        block_brick, velocity, pressure, cell_visc, cell_dens
    )
    marker_visc, moments = marker_call(block_counts, positions, start_visc, marker_dens, bricks)
    visc_next, dens_next = moments_call(moments, ids, cell_visc, cell_dens)
    return velocity_next, pressure_next, visc_next, dens_next, marker_visc


def solution(mesh):
    in_specs = (
        P(None, "grid", "mark", None),
        P("grid", "mark", None),
        P("grid", "mark", None),
        P("grid", "mark", None),
        P(("grid", "mark"), None),
        P(("grid", "mark"), None),
        P(("grid", "mark"), None, None, None),
        P(("grid", "mark"), None, None),
        P(("grid", "mark"), None, None),
    )
    out_specs = (
        P(None, "grid", "mark", None),
        P("grid", "mark", None),
        P("grid", "mark", None),
        P("grid", "mark", None),
        P(("grid", "mark"), None, None),
    )
    return jax.shard_map(
        per_device, mesh=mesh, in_specs=in_specs, out_specs=out_specs, check_vma=False
    )
```

time: 1050 us -> 124 us (0.12)
  the two profiles are of different devices: /device:TPU:38 before, /device:TPU:7 now
where the time goes in v1:
time: 124 us
  Pallas kernels  116 us (94%)
  local copies, waits for them, and re-layouts  7.37 us (6%)
    pallas_call x1, Pallas kernels, grid_call(): pl.pallas_call(grid_kernel, out_shape=(jax.ShapeDtypeStruct((OWNERS, 8, 1...  52.6 us
    pallas_call x1, Pallas kernels, moments_call(): pl.pallas_call(moments_kernel, out_shape=(field, field), in_specs=[hbm, v...  50.2 us
    pallas_call x1, Pallas kernels, marker_call(): pl.pallas_call(marker_kernel, out_shape=(jax.ShapeDtypeStruct((OWNERS, CA...  12.8 us
    unnamed x24, local copies, waits for them, and re-layouts  7.37 us

profile of v1, /device:TPU:7, one launch (start us, length us, event | category | flops | bytes accessed | tf_op | source)
XLA Modules:
  0.0 123.6 jit_solution(10392077483419851511)
XLA Ops:
  0.6 0.0 copy-start
  0.6 1.0 copy-done
  1.7 0.0 copy-start.2
  1.7 1.0 copy-done.2
  2.7 0.0 copy-start.6
  2.7 1.0 copy-done.6
  3.8 0.0 copy-start.7
  3.8 0.7 copy-done.7
  4.5 0.0 copy-start.4
  4.5 0.0 copy-start.5
  4.5 0.0 copy-start.8
  4.5 52.6 %grid_step.1 = (f32[16,8,128]{2,1,0:T(8,128)S(1)}, f32[16,48,384]{2,1,0:T(8,128)S(1)}, f32[3,32,16,256]{3,2,1,0:T(8,128)}, f32[32,16,256]{2,1,0:T(8,128)S(1)}) custom-call(s32[16,48]{1,0:T(8,128)S(1)} %copy-done.7, f32[3,32,16,256]{3,2,1,0:T(8,128)} %velocity.1, f32[32,16,256]{2,1,0:T(8,128)S(1)} %copy-done.6, f32[32,16,256]{2,1,0:T(8,128)S(1)} %copy-done, ...), custom_call_target="tpu_custom_call" | custom-call | tf_op jit(solution)/shard_map/grid_step/pallas_call | solution.py:523
  57.0 0.0 copy-done.4
  57.0 0.0 copy-done.5
  57.1 0.0 copy-done.8
  57.1 0.0 copy-start.1
  57.1 0.0 copy-start.3
  57.1 12.8 %markers.1 = (f32[16,48,256]{2,1,0:T(8,128)}, f32[16,48,384]{2,1,0:T(8,128)S(1)}) custom-call(s32[1,16]{1,0:T(1,128)S(1)} %copy-done.8, f32[16,3,48,256]{3,2,1,0:T(8,128)} %pos.1, f32[16,48,256]{2,1,0:T(8,128)S(1)} %copy-done.4, f32[16,48,256]{2,1,0:T(8,128)S(1)} %copy-done.5, f32[16,48,384]{2,1,0:T(8,128)S(1)} %get-tuple-element.15.bricks), custom_call_target="tpu_custom_call" | custom-call | tf_op jit(solution)/shard_map/markers/pallas_call | solution.py:215
  69.9 0.0 copy-start.9
  69.9 0.0 copy-done.1
  69.9 0.0 copy-done.3
  69.9 50.2 %moments_home.1 = (f32[32,16,256]{2,1,0:T(8,128)S(1)}, f32[32,16,256]{2,1,0:T(8,128)S(1)}) custom-call(f32[16,48,384]{2,1,0:T(8,128)S(1)} %get-tuple-element.16.moments, f32[16,8,128]{2,1,0:T(8,128)S(1)} %get-tuple-element.17.ids, f32[32,16,256]{2,1,0:T(8,128)S(1)} %copy-done.1, f32[32,16,256]{2,1,0:T(8,128)S(1)} %copy-done.3), custom_call_target="tpu_custom_call" | custom-call | tf_op jit(solution)/shard_map/moments_home/pallas_call | solution.py:684
  120.1 0.0 copy-done.9
  120.1 1.1 copy.18
  121.3 0.8 copy.19
  122.1 0.8 copy.20
  122.8 0.8 copy.21
Async XLA Ops:
  0.6 1.0 copy-start
  1.7 1.0 copy-start.2
  2.7 1.0 copy-start.6
  3.8 0.7 copy-start.7
  4.5 52.6 %copy-start.4 = (f32[16,48,256]{2,1,0:T(8,128)S(1)}, f32[16,48,256]{2,1,0:T(8,128)}, u32[]{:S(2)}) copy-start(f32[16,48,256]{2,1,0:T(8,128)} %visc.4) | copy-start | bytes 2359300
  4.5 52.6 %copy-start.5 = (f32[16,48,256]{2,1,0:T(8,128)S(1)}, f32[16,48,256]{2,1,0:T(8,128)}, u32[]{:S(2)}) copy-start(f32[16,48,256]{2,1,0:T(8,128)} %dens.4) | copy-start | bytes 2359300
  4.5 52.6 %copy-start.8 = (s32[1,16]{1,0:T(1,128)S(1)}, s32[1,16]{1,0:T(1,128)}, u32[]{:S(2)}) copy-start(s32[1,16]{1,0:T(1,128)} %counts.1) | copy-start | bytes 196
  57.1 12.8 %copy-start.1 = (f32[32,16,256]{2,1,0:T(8,128)S(1)}, f32[32,16,256]{2,1,0:T(8,128)}, u32[]{:S(2)}) copy-start(f32[32,16,256]{2,1,0:T(8,128)} %visc.5) | copy-start | bytes 1572868
  57.1 12.8 %copy-start.3 = (f32[32,16,256]{2,1,0:T(8,128)S(1)}, f32[32,16,256]{2,1,0:T(8,128)}, u32[]{:S(2)}) copy-start(f32[32,16,256]{2,1,0:T(8,128)} %dens.5) | copy-start | bytes 1572868
  69.9 50.2 %copy-start.9 = (f32[3,32,16,256]{3,2,1,0:T(8,128)S(1)}, f32[3,32,16,256]{3,2,1,0:T(8,128)}, u32[]{:S(2)}) copy-start(f32[3,32,16,256]{3,2,1,0:T(8,128)} %get-tuple-element.26) | copy-start | bytes 4718596

commit v2 on v1

v2 whole, which is shorter than its diff:
```python
import functools
import math
import jax
import jax.numpy as jnp
from jax import lax
from jax.sharding import PartitionSpec as P
from jax.experimental import pallas as pl
from jax.experimental.pallas import tpu as pltpu

F32, BF16 = jnp.float32, jnp.bfloat16
VMEM = pltpu.VMEM
CAP, BLOCK, OWNERS = 48, 256, 16
NT = (((1,), (1,)), ((), ()))
GROUPS = 6


def split(x):
    hi = x.astype(BF16)
    return hi, (x - hi.astype(F32)).astype(BF16)


def axis_weights(fraction, cells):
    half = 0.5 * cells
    factor = jnp.exp(2.0 * cells * fraction - 2.0 * half)
    centres = [i + 0.5 - half for i in range(cells)]
    powers = [None, factor]
    for i in range(2, cells):
        powers.append(powers[i // 2] * powers[i - i // 2])
    raw = [jnp.full_like(factor, math.exp(-centres[0] ** 2))]
    raw += [math.exp(-(centres[i] ** 2)) * powers[i] for i in range(1, cells)]
    total = functools.reduce(jnp.add, raw)
    scale = 1.0 / total
    weights = [r * scale for r in raw]
    mean = functools.reduce(jnp.add, [c * w for c, w in zip(centres, weights)])
    return weights, mean


def masks():
    sub = lax.broadcasted_iota(jnp.int32, (8, 128), 0)
    lane = lax.broadcasted_iota(jnp.int32, (8, 128), 1)
    sub2 = lax.broadcasted_iota(jnp.int32, (8, 256), 0)
    return sub, lane, sub2, sub < 4, sub2 < 4


def both(x, low):
    turned = pltpu.roll(x, 4, 0)
    return jnp.where(low, x, turned), jnp.where(low, turned, x)


def fold(a, b, low):
    return jnp.where(low, a, b) + pltpu.roll(jnp.where(low, b, a), 4, 0)


def skew(x, sub, sign):
    out = x
    for s in range(1, 4):
        out = jnp.where(sub % 4 == s, pltpu.roll(x, (sign * 32 * s) % 128, 1), out)
    return out


def pieces(tiles):
    his, los = [], []
    for n in range(0, len(tiles), 2):
        hi, lo = split(jnp.concatenate(tiles[n : n + 2], axis=0))
        his.append(hi)
        los.append(lo)
    return jnp.concatenate(his + los, axis=0)


def prepare(q, k, row, u, pos, bricks, wz_s, wy_s, planes):
    rows = pl.ds(row, 8)
    sub, lane, sub2, low, low2 = masks()
    wx, mean_x = axis_weights(pos[q, 0, rows, :], 4)
    wy, mean_y = axis_weights(pos[q, 1, rows, :], 4)
    wz, mean_z = axis_weights(pos[q, 2, rows, :], 8)
    for h in range(2):
        part = slice(128 * h, 128 * h + 128)
        for n in range(8):
            wz_s[u, h, pl.ds(8 * n, 8), :] = wz[n][:, part]
        for j in range(4):
            wy_s[u, h, pl.ds(8 * j, 8), :] = wy[j][:, part]
    for b in range(8):
        for h in range(2):
            col = wz_s[u, h, pl.ds(b, 8, stride=8), :]
            for jp in range(2):
                pair = [
                    col * jnp.broadcast_to(wy_s[u, h, pl.ds(8 * j + b, 1), :], (8, 128))
                    for j in (2 * jp, 2 * jp + 1)
                ]
                hi, lo = split(jnp.concatenate(pair, axis=0))
                at = 32 * (b % 4) + 16 * jp
                planes[u, b // 4, pl.ds(at, 16), pl.ds(128 * h, 128)] = hi
                planes[u, b // 4, pl.ds(128 + at, 16), pl.ds(128 * h, 128)] = lo

    diag = (lane // 32) == (sub % 4)
    turned_i = (lane // 32 + 4 - sub % 4) % 4
    c_i = turned_i.astype(F32) - 1.5
    c_j = ((lane // 8) % 4).astype(F32) - 1.5
    c_k = (lane % 8).astype(F32) - 3.5
    v = [both(skew(bricks[k, rows, pl.ds(128 * c, 128)], sub, 1), low) for c in range(3)]
    lefts = []
    for side in range(2):
        vx, vy, vz = [x[side] for x in v]
        kinds = [
            vx, vy, vz, c_j * vy, c_k * vz,
            c_j * vx + c_i * vy, c_k * vx + c_i * vz, c_k * vy + c_j * vz,
        ]
        tiles = []
        for kind in kinds:
            turned = [kind] + [pltpu.roll(kind, 128 - 32 * i, 1) for i in range(1, 4)]
            for ip in range(2):
                tile = jnp.where(low, turned[2 * ip], turned[2 * ip + 1])
                tiles.append(jnp.where(diag, tile, 0.0))
        lefts.append(pieces(tiles))
    pairs = ([], [])
    for ip in range(2):
        first, second = both(wx[2 * ip], low2), both(wx[2 * ip + 1], low2)
        for side in range(2):
            pairs[side].append(jnp.where(low2, first[side], second[side]))
    return lefts, pairs, (mean_x, mean_y, mean_z)


def strain(q, k, row, u, prepared, visc, dens, marker_out, count, planes):
    rows = pl.ds(row, 8)
    sub, lane, sub2, low, low2 = masks()
    lefts, pairs, (mean_x, mean_y, mean_z) = prepared
    results = []
    for side in range(2):
        left = jnp.concatenate([lefts[side], lefts[side]], axis=1)
        out = jnp.dot(left, planes[u, side], preferred_element_type=F32)
        results.append(out[:128] + out[128:])
    centred = [
        [pairs[side][ip] * jnp.where(low2, 2 * ip - 1.5, 2 * ip - 0.5) for ip in range(2)]
        for side in range(2)
    ]

    def along_x(kind, weights):
        at = 16 * kind
        sums = [
            results[side][at : at + 8] * weights[side][0]
            + results[side][at + 8 : at + 16] * weights[side][1]
            for side in range(2)
        ]
        return fold(*sums, low2)

    vx, vy, vz, yy, zz, xy, xz, yz = [along_x(n, pairs) for n in range(8)]
    xx = along_x(0, centred) - mean_x * vx
    yy = yy - mean_y * vy
    zz = zz - mean_z * vz
    xy = xy - mean_y * vx - mean_x * vy
    xz = xz - mean_z * vx - mean_x * vz
    yz = yz - mean_z * vy - mean_y * vz
    invariant = 2.0 * (xx * xx + yy * yy + zz * zz) + xy * xy + xz * xz + yz * yz
    shift = jnp.log(1.0 + invariant * 4.0) * (1.0 / 3.0)
    start = visc[q, rows, :]
    live = (sub2 + row) < count
    weakened = start * jnp.exp(-shift)
    marker_out[k, rows, :] = jnp.where(live, weakened, 0.0)
    carried = [
        jnp.where(live, 1.0, 0.0),
        jnp.where(live, jnp.log(weakened), 0.0),
        jnp.where(live, dens[q, rows, :], 0.0),
    ]
    carried = [both(c, low2) for c in carried]
    return [
        pieces([carried[m][side] * pairs[side][ip] for m in range(3) for ip in range(2)])
        for side in range(2)
    ]


def deposit(k, row, u, lefts, moments, planes):
    rows = pl.ds(row, 8)
    sub, lane, sub2, low, low2 = masks()
    diag = (lane // 32) == (sub % 4)
    sums = []
    for side in range(2):
        out = lax.dot_general(lefts[side], planes[u, side], NT, preferred_element_type=F32)
        sums.append(out[:48, :128] + out[:48, 128:] + out[48:, :128])
    for m in range(3):
        halves = []
        for side in range(2):
            p = [jnp.where(diag, sums[side][16 * m + 8 * ip : 16 * m + 8 * ip + 8], 0.0) for ip in range(2)]
            halves.append(
                jnp.where(low, p[0], pltpu.roll(p[0], 32, 1))
                + jnp.where(low, pltpu.roll(p[1], 64, 1), pltpu.roll(p[1], 96, 1))
            )
        moments[k, rows, pl.ds(128 * m, 128)] = skew(fold(*halves, low), sub, -1)


NX_L, NY_L, NZ = 32, 16, 256
BRICKS = 1024
MESH = pl.DeviceIdType.MESH
SWEEPS = 4
relax_weight = 0.6
pressure_rate = 0.25
gravity = 1.0


def group_transpose(tiles, group):
    tiles = list(tiles)
    for d in (8, 4, 2, 1):
        upper = (group & d) != 0
        for t in range(16):
            if t & d == 0:
                a, b = tiles[t], tiles[t + d]
                tiles[t] = jnp.where(upper, pltpu.roll(b, 8 * d, 1), a)
                tiles[t + d] = jnp.where(upper, b, pltpu.roll(a, 128 - 8 * d, 1))
    return tiles


def peers():
    g, me = lax.axis_index("grid"), lax.axis_index("mark")

    def after(k):
        return lax.rem(me + k, OWNERS)

    def before(k):
        return lax.rem(me + OWNERS - k, OWNERS)

    return g, me, after, before


def remote(src, dst, send, recv, device):
    return pltpu.make_async_remote_copy(
        src_ref=src, dst_ref=dst, send_sem=send, recv_sem=recv, device_id=device, device_id_type=MESH
    )


def step_kernel(
    counts, brick_ids, velocity, pressure, visc, dens, positions, start_visc, marker_dens,
    velocity_out, pressure_out, visc_out, dens_out, marker_out,
    state_a, state_b, visc_s, dens_s, halves, planes_hi, planes_lo, one_hot, ids_send, ids_recv,
    brick_send, bricks, kx, kym, kyp, kzm, kzp, damp, x_lo, x_hi, face_lo, face_hi, y_lo, y_hi,
    vx_lo, vx_hi, vface_lo, vface_hi, vy_lo, vy_hi, pos, mvisc, mdens, marker_s, moments, arrived,
    wz_s, wy_s, planes, hits, hi_s, lo_s, sums, cells,
    load_sem, id_send, id_recv, b_send, b_recv, h_send, h_recv, v_send, v_recv, m_send, m_recv, out_sem,
):
    g, me, after, before = peers()
    ahead, behind = lax.rem(g + 1, 8), lax.rem(g + 7, 8)
    loads = [
        pltpu.make_async_copy(velocity, state_a.at[pl.ds(0, 3), pl.ds(1, NX_L)], load_sem.at[0]),
        pltpu.make_async_copy(pressure, state_a.at[3, pl.ds(1, NX_L)], load_sem.at[1]),
        pltpu.make_async_copy(visc, visc_s.at[pl.ds(1, NX_L)], load_sem.at[2]),
        pltpu.make_async_copy(dens, dens_s, load_sem.at[3]),
    ]
    marker_loads = [
        pltpu.make_async_copy(positions, pos, load_sem.at[4]),
        pltpu.make_async_copy(start_visc, mvisc, load_sem.at[7]),
        pltpu.make_async_copy(marker_dens, mdens, load_sem.at[8]),
    ]
    for c in loads + marker_loads:
        c.start()
    barrier = pltpu.get_barrier_semaphore()
    for k in range(1, OWNERS):
        pl.semaphore_signal(barrier, inc=1, device_id=(g, after(k)), device_id_type=MESH)
    pl.semaphore_signal(barrier, inc=1, device_id=(ahead, me), device_id_type=MESH)
    pl.semaphore_signal(barrier, inc=1, device_id=(behind, me), device_id_type=MESH)

    number = brick_ids[...]
    number = (((number >> 5) & 3) * 32 + (number & 31)) * 8 + (number >> 7)
    number = number.astype(F32)
    ids_send[...] = jnp.full((OWNERS, 8, 128), -1.0, F32)
    for q in range(OWNERS):
        ids_send[q, :, pl.ds(0, CAP)] = jnp.broadcast_to(number[q : q + 1], (8, CAP))
    pl.semaphore_wait(barrier, OWNERS + 1)

    def send_ids(k, _):
        remote(ids_send.at[after(k)], ids_recv.at[k], id_send.at[k], id_recv.at[k], (g, after(k))).start()
        return 0

    lax.fori_loop(1, OWNERS, send_ids, 0)
    ids_recv[0] = ids_send[me]
    for c in loads:
        c.wait()

    def halo(n, state):
        return [
            remote(state.at[:, 1], x_hi.at[n], h_send.at[n, 0], h_recv.at[n, 0], (behind, me)),
            remote(state.at[:, NX_L], x_lo.at[n], h_send.at[n, 1], h_recv.at[n, 1], (ahead, me)),
            remote(face_lo.at[n], y_hi.at[n], h_send.at[n, 2], h_recv.at[n, 2], (g, before(1))),
            remote(face_hi.at[n], y_lo.at[n], h_send.at[n, 3], h_recv.at[n, 3], (g, after(1))),
        ]

    def first_faces(x, _):
        face_lo[0, x] = jnp.concatenate([state_a[c, x + 1, 0:1, :] for c in range(4)], axis=0)
        face_hi[0, x] = jnp.concatenate([state_a[c, x + 1, 15:16, :] for c in range(4)], axis=0)
        return 0

    lax.fori_loop(0, NX_L, first_faces, 0)
    for x in range(NX_L):
        vface_lo[x : x + 1, :] = visc_s[x + 1, 0:1, :]
        vface_hi[x : x + 1, :] = visc_s[x + 1, 15:16, :]
    visc_halo = [
        remote(visc_s.at[1], vx_hi, v_send.at[0], v_recv.at[0], (behind, me)),
        remote(visc_s.at[NX_L], vx_lo, v_send.at[1], v_recv.at[1], (ahead, me)),
        remote(vface_lo, vy_hi, v_send.at[2], v_recv.at[2], (g, before(1))),
        remote(vface_hi, vy_lo, v_send.at[3], v_recv.at[3], (g, after(1))),
    ]
    for c in halo(0, state_a) + visc_halo:
        c.start()

    def to_halves(x, _):
        for c in range(3):
            plane = state_a[c, x + 1]
            at = pl.multiple_of(c * 512 + x * 16, 16)
            for h in range(2):
                halves[h, pl.ds(at, 16), :] = plane[:, 128 * h : 128 * h + 128]
        return 0

    lax.fori_loop(0, NX_L, to_halves, 0)
    group = lax.broadcasted_iota(jnp.int32, (8, 128), 1) // 8

    def to_bricks(n, _):
        bj, h = n // 2, lax.rem(n, 2)
        for c in range(3):
            tiles = [
                halves[h, pl.ds(c * 512 + 16 * i + 4 * bj + j, 8, stride=64), :]
                for i in range(4)
                for j in range(4)
            ]
            tiles = group_transpose(tiles, group)
            for t in range(0, 16, 2):
                hi, lo = split(jnp.concatenate(tiles[t : t + 2], axis=0))
                at = pl.multiple_of((bj * 32 + h * 16 + t) * 8, 16)
                planes_hi[pl.ds(at, 16), pl.ds(128 * c, 128)] = hi
                planes_lo[pl.ds(at, 16), pl.ds(128 * c, 128)] = lo
        return 0

    lax.fori_loop(0, 8, to_bricks, 0)

    def wait_ids(k, _):
        remote(ids_send.at[after(k)], ids_recv.at[k], id_send.at[k], id_recv.at[k], (g, after(k))).wait()
        return 0

    lax.fori_loop(1, OWNERS, wait_ids, 0)

    def brick_copy(k):
        return remote(
            brick_send.at[k], bricks.at[k], b_send.at[k], b_recv.at[k], (g, before(k))
        )

    lanes = lax.broadcasted_iota(jnp.int32, (CAP, 128), 1).astype(F32)

    def gather(n, _):
        for m in range(4):
            column = jnp.transpose(jnp.broadcast_to(ids_recv[4 * n + m][0:1, :], (128, 128)))[:CAP]
            for t in range(8):
                hit = jnp.where(column == lanes + 128.0 * t, 1.0, 0.0).astype(BF16)
                one_hot[pl.ds(CAP * m, CAP), pl.ds(128 * t, 128)] = hit
        found = jnp.dot(one_hot[...], planes_hi[...], preferred_element_type=F32)
        found = found + jnp.dot(one_hot[...], planes_lo[...], preferred_element_type=F32)
        for m in range(4):
            brick_send[4 * n + m] = found[CAP * m : CAP * m + CAP]
        for m in range(4):
            k = 4 * n + m

            @pl.when(k > 0)
            def _():
                brick_copy(k).start()

        return 0

    lax.fori_loop(0, 4, gather, 0)
    bricks[0] = brick_send[0]
    for c in marker_loads:
        c.wait()

    def moment_copy(k):
        return remote(moments.at[k], arrived.at[k], m_send.at[k], m_recv.at[k], (g, after(k)))

    def marker_store(k):
        return pltpu.make_async_copy(marker_s.at[k], marker_out.at[after(k)], out_sem.at[k])

    def owner_markers(k, _):
        q = after(k)
        count = counts[0, q]

        @pl.when(k > 0)
        def _():
            brick_copy(k).wait()

        ready, spread = {}, {}
        for t in range(GROUPS + 2):
            if t < GROUPS:
                ready[t] = prepare(q, k, 8 * t, t, pos, bricks, wz_s, wy_s, planes)
            u = t - 1
            if 0 <= u < GROUPS:
                spread[u] = strain(q, k, 8 * u, u, ready.pop(u), mvisc, mdens, marker_s, count, planes)
            u = t - 2
            if 0 <= u < GROUPS:
                deposit(k, 8 * u, u, spread.pop(u), moments, planes)
        marker_store(k).start()

        @pl.when(k > 0)
        def _():
            moment_copy(k).start()

        return 0

    lax.fori_loop(0, 1, owner_markers, 0)

    x_lo_on = (g > 0).astype(F32)
    x_hi_on = (g < 7).astype(F32)
    y_lo_on = (me > 0).astype(F32)
    y_hi_on = (me < OWNERS - 1).astype(F32)
    row = lax.broadcasted_iota(jnp.int32, (NY_L, NZ), 0)
    col = lax.broadcasted_iota(jnp.int32, (NY_L, NZ), 1)
    first_y, last_y = row == 0, row == NY_L - 1
    first_z, last_z = col == 0, col == NZ - 1

    def y_minus(plane, edge):
        return jnp.where(first_y, jnp.broadcast_to(edge, plane.shape), pltpu.roll(plane, 1, 0))

    def y_plus(plane, edge):
        return jnp.where(last_y, jnp.broadcast_to(edge, plane.shape), pltpu.roll(plane, NY_L - 1, 0))

    def z_minus(plane):
        return jnp.where(first_z, 0.0, pltpu.roll(plane, 1, 1))

    def z_plus(plane):
        return jnp.where(last_z, 0.0, pltpu.roll(plane, NZ - 1, 1))

    for c in visc_halo:
        c.wait()
    visc_s[0] = vx_lo[...] * x_lo_on
    visc_s[NX_L + 1] = vx_hi[...] * x_hi_on

    def couplings(x, _):
        here, below, above = visc_s[x + 1], visc_s[x], visc_s[x + 2]
        k_xm, k_xp = 0.5 * (here + below), 0.5 * (here + above)
        k_ym = 0.5 * (here + y_minus(here, vy_lo[pl.ds(x, 1), :] * y_lo_on))
        k_yp = 0.5 * (here + y_plus(here, vy_hi[pl.ds(x, 1), :] * y_hi_on))
        k_zm, k_zp = 0.5 * (here + z_minus(here)), 0.5 * (here + z_plus(here))
        kx[x] = k_xm
        kx[x + 1] = k_xp
        kym[x] = k_ym
        kyp[x] = k_yp
        kzm[x] = k_zm
        kzp[x] = k_zp
        damp[x] = relax_weight / (k_xm + k_xp + k_ym + k_yp + k_zm + k_zp)
        return 0

    lax.fori_loop(0, NX_L, couplings, 0)

    for n in range(SWEEPS):
        old, new = (state_a, state_b) if n % 2 == 0 else (state_b, state_a)
        for c in halo(n, old):
            c.wait()
        old[:, 0] = x_lo[n] * x_lo_on
        old[:, NX_L + 1] = x_hi[n] * x_hi_on

        def sweep(x, _, n=n, old=old, new=new):
            low = y_lo[n, x] * y_lo_on
            high = y_hi[n, x] * y_hi_on
            press = old[3, x + 1]
            press_near = [
                old[3, x],
                y_minus(press, low[3:4]),
                z_minus(press),
            ]
            weights = [kx[x + 1], kx[x], kyp[x], kym[x], kzp[x], kzm[x]]
            scale = damp[x]
            divergence = jnp.zeros_like(press)
            fresh = []
            for c in range(3):
                v = old[c, x + 1]
                near = [
                    old[c, x + 2],
                    old[c, x],
                    y_plus(v, high[c : c + 1]),
                    y_minus(v, low[c : c + 1]),
                    z_plus(v),
                    z_minus(v),
                ]
                forcing = press_near[c] - press
                for w, s in zip(weights, near):
                    forcing = forcing + w * (s - v)
                if c == 2:
                    forcing = forcing - gravity * dens_s[x]
                fresh.append(v + scale * forcing)
                divergence = divergence + (near[2 * c] - v)
            fresh.append(press - pressure_rate * visc_s[x + 1] * divergence)
            for c in range(4):
                new[c, x + 1] = fresh[c]
            if n + 1 < SWEEPS:
                face_lo[n + 1, x] = jnp.concatenate([f[0:1] for f in fresh], axis=0)
                face_hi[n + 1, x] = jnp.concatenate([f[15:16] for f in fresh], axis=0)
            return 0

        lax.fori_loop(0, NX_L, sweep, 0)
        if n + 1 < SWEEPS:
            for c in halo(n + 1, new):
                c.start()
        if n + 1 < SWEEPS:
            lax.fori_loop(1 + 5 * n, 6 + 5 * n, owner_markers, 0)
    last = state_a if SWEEPS % 2 == 0 else state_b
    stores = [
        pltpu.make_async_copy(last.at[pl.ds(0, 3), pl.ds(1, NX_L)], velocity_out, load_sem.at[5]),
        pltpu.make_async_copy(last.at[3, pl.ds(1, NX_L)], pressure_out, load_sem.at[6]),
    ]
    for c in stores:
        c.start()
    arrived[0] = moments[0]

    lane = lax.broadcasted_iota(jnp.int32, (8, 128), 1)
    rows = [jnp.full((8, 128), -1.0, F32) for _ in range(6)]
    for k in range(OWNERS):
        at = CAP * k
        t, off = at // 128, at % 128
        tile = ids_recv[k]
        turned = pltpu.roll(tile, off, 1) if off else tile
        rows[t] = jnp.where((lane >= off) & (lane < off + CAP), turned, rows[t])
        over = off + CAP - 128
        if over > 0:
            rows[t + 1] = jnp.where(lane < over, turned, rows[t + 1])

    wide = [jnp.concatenate([r, r], axis=0) for r in rows]
    sub = lax.broadcasted_iota(jnp.int32, (16, 128), 0).astype(F32)

    def mark_hits(r, _):
        at = pl.multiple_of(r * 16, 16)
        here = sub + (r * 16).astype(F32)
        for t in range(6):
            hits[pl.ds(at, 16), pl.ds(128 * t, 128)] = jnp.where(wide[t] == here, 1.0, 0.0).astype(BF16)
        return 0

    lax.fori_loop(0, BRICKS // 16, mark_hits, 0)

    def arrive(k, _):
        moment_copy(k).wait()
        return 0

    lax.fori_loop(1, OWNERS, arrive, 0)

    def moment_pieces(k, _):
        hi, lo = split(arrived[k])
        at = pl.multiple_of(k * CAP, 16)
        hi_s[pl.ds(at, CAP), :] = hi
        lo_s[pl.ds(at, CAP), :] = lo
        return 0

    lax.fori_loop(0, OWNERS, moment_pieces, 0)

    def scatter(n, _):
        at = pl.ds(pl.multiple_of(n * 256, 256), 256)
        block = hits[at, :]
        total = jnp.dot(block, hi_s[...], preferred_element_type=F32)
        total = total + jnp.dot(block, lo_s[...], preferred_element_type=F32)
        for m in range(3):
            sums[m, at, :] = total[:, 128 * m : 128 * m + 128]
        return 0

    lax.fori_loop(0, 4, scatter, 0)
    def to_cells(n, _):
        bj, h = n // 2, lax.rem(n, 2)
        for m in range(3):
            tiles = [
                sums[m, pl.ds(pl.multiple_of((bj * 32 + h * 16 + t) * 8, 8), 8), :] for t in range(16)
            ]
            tiles = group_transpose(tiles, group)
            for i in range(4):
                for j in range(4):
                    cells[m, h, pl.ds(16 * i + 4 * bj + j, 8, stride=64), :] = tiles[4 * i + j]
        return 0

    lax.fori_loop(0, 8, to_cells, 0)

    def finish(x, _):
        at = pl.ds(pl.multiple_of(x * 16, 16), 16)
        for h in range(2):
            part = pl.ds(128 * h, 128)
            below = 1.0 / (cells[0, h, at, :] + 1.0)
            visc_out[x, :, part] = jnp.exp((cells[1, h, at, :] + jnp.log(visc_s[x + 1, :, part])) * below)
            dens_out[x, :, part] = (cells[2, h, at, :] + dens_s[x, :, part]) * below
        return 0

    lax.fori_loop(0, NX_L, finish, 0)

    def wait_markers(k, _):
        marker_store(k).wait()
        return 0

    lax.fori_loop(0, OWNERS, wait_markers, 0)
    for c in stores:
        c.wait()


def per_device(
    velocity, pressure, cell_visc, cell_dens, block_brick, block_counts, positions, start_visc, marker_dens
):
    vm = pl.BlockSpec(memory_space=pltpu.VMEM)
    hbm = pl.BlockSpec(memory_space=pl.ANY)
    dma = pltpu.SemaphoreType.DMA
    field = (NX_L, NY_L, NZ)
    padded = (NX_L + 2, NY_L, NZ)
    shape = jax.ShapeDtypeStruct
    return pl.pallas_call(
        step_kernel,
        out_shape=(
            shape((3,) + field, F32),
            shape(field, F32),
            shape(field, F32),
            shape(field, F32),
            shape((OWNERS, CAP, BLOCK), F32),
        ),
        in_specs=[pl.BlockSpec(memory_space=pltpu.SMEM), vm] + [hbm] * 7,
        out_specs=(hbm, hbm, vm, vm, hbm),
        scratch_shapes=[
            VMEM((4,) + padded, F32),
            VMEM((4,) + padded, F32),
            VMEM(padded, F32),
            VMEM(field, F32),
            VMEM((2, 1536, 128), F32),
            VMEM((BRICKS, 384), BF16),
            VMEM((BRICKS, 384), BF16),
            VMEM((4 * CAP, BRICKS), BF16),
            VMEM((OWNERS, 8, 128), F32),
            VMEM((OWNERS, 8, 128), F32),
            VMEM((OWNERS, CAP, 384), F32),
            VMEM((OWNERS, CAP, 384), F32),
            VMEM((NX_L + 1, NY_L, NZ), F32),
            VMEM(field, F32),
            VMEM(field, F32),
            VMEM(field, F32),
            VMEM(field, F32),
            VMEM(field, F32),
            VMEM((SWEEPS, 4, NY_L, NZ), F32),
            VMEM((SWEEPS, 4, NY_L, NZ), F32),
            VMEM((SWEEPS, NX_L, 4, NZ), F32),
            VMEM((SWEEPS, NX_L, 4, NZ), F32),
            VMEM((SWEEPS, NX_L, 4, NZ), F32),
            VMEM((SWEEPS, NX_L, 4, NZ), F32),
            VMEM((NY_L, NZ), F32),
            VMEM((NY_L, NZ), F32),
            VMEM((NX_L, NZ), F32),
            VMEM((NX_L, NZ), F32),
            VMEM((NX_L, NZ), F32),
            VMEM((NX_L, NZ), F32),
            VMEM((OWNERS, 3, CAP, BLOCK), F32),
            VMEM((OWNERS, CAP, BLOCK), F32),
            VMEM((OWNERS, CAP, BLOCK), F32),
            VMEM((OWNERS, CAP, BLOCK), F32),
            VMEM((OWNERS, CAP, 384), F32),
            VMEM((OWNERS, CAP, 384), F32),
            VMEM((GROUPS, 2, 64, 128), F32),
            VMEM((GROUPS, 2, 32, 128), F32),
            VMEM((GROUPS, 2, 256, 256), BF16),
            VMEM((BRICKS, OWNERS * CAP), BF16),
            VMEM((OWNERS * CAP, 384), BF16),
            VMEM((OWNERS * CAP, 384), BF16),
            VMEM((3, BRICKS, 128), F32),
            VMEM((3, 2, 512, 128), F32),
            dma((9,)),
            dma((OWNERS,)),
            dma((OWNERS,)),
            dma((OWNERS,)),
            dma((OWNERS,)),
            dma((SWEEPS, 4)),
            dma((SWEEPS, 4)),
            dma((4,)),
            dma((4,)),
            dma((OWNERS,)),
            dma((OWNERS,)),
            dma((OWNERS,)),
        ],
        compiler_params=pltpu.CompilerParams(
            collective_id=0, has_side_effects=True, vmem_limit_bytes=56 << 20
        ),
        name="step",
    )(
        block_counts, block_brick, velocity, pressure, cell_visc, cell_dens,
        positions, start_visc, marker_dens,
    )


def solution(mesh):
    in_specs = (
        P(None, "grid", "mark", None),
        P("grid", "mark", None),
        P("grid", "mark", None),
        P("grid", "mark", None),
        P(("grid", "mark"), None),
        P(("grid", "mark"), None),
        P(("grid", "mark"), None, None, None),
        P(("grid", "mark"), None, None),
        P(("grid", "mark"), None, None),
    )
    out_specs = (
        P(None, "grid", "mark", None),
        P("grid", "mark", None),
        P("grid", "mark", None),
        P("grid", "mark", None),
        P(("grid", "mark"), None, None),
    )
    return jax.shard_map(
        per_device, mesh=mesh, in_specs=in_specs, out_specs=out_specs, check_vma=False
    )
```

time: 124 us -> 81.9 us (0.66)
  the two profiles are of different devices: /device:TPU:7 before, /device:TPU:38 now
where the time goes in v2:
time: 81.9 us; the launch traced here: 80.6 us
  Pallas kernels  73.9 us (90%)
  local copies, waits for them, and re-layouts  6.03 us (7%)
    pallas_call x1, Pallas kernels, per_device(): pl.pallas_call(step_kernel, out_shape=(shape((3,) + field, F32), shape(fi...  73.9 us
    unnamed x13, local copies, waits for them, and re-layouts  6.03 us

profile of v2, /device:TPU:38, one launch (start us, length us, event | category | flops | bytes accessed | tf_op | source)
XLA Modules:
  0.0 80.6 jit_solution(18037071910966533027)
XLA Ops:
  0.6 73.9 %step.1 = (f32[3,32,16,256]{3,2,1,0:T(8,128)}, f32[32,16,256]{2,1,0:T(8,128)}, f32[32,16,256]{2,1,0:T(8,128)}, f32[32,16,256]{2,1,0:T(8,128)}, f32[16,48,256]{2,1,0:T(8,128)}) custom-call(s32[1,16]{1,0:T(1,128)} %counts.1, s32[16,48]{1,0:T(8,128)} %brick_ids.1, f32[3,32,16,256]{3,2,1,0:T(8,128)} %velocity.1, f32[32,16,256]{2,1,0:T(8,128)} %pressure.1, ...), custom_call_target="tpu_custom_call" | custom-call | tf_op jit(solution)/shard_map/step/pallas_call | solution.py:597
  74.6 0.0 copy-start.3
  74.6 0.0 copy-start.2
  74.6 2.8 %copy.19 = f32[3,32,16,256]{3,2,1,0:T(8,128)} copy(f32[3,32,16,256]{3,2,1,0:T(8,128)} %get-tuple-element.10) | data formatting | bytes 3145728
  77.3 0.0 copy-done.3
  77.3 0.0 copy-start.1
  77.3 0.0 copy-start
  77.3 0.8 copy.20
  78.1 0.0 copy-done.2
  78.1 0.8 copy.21
  78.9 0.0 copy-done.1
  78.9 0.8 copy.22
  79.7 0.0 copy-done
  79.7 0.9 %copy.23 = f32[16,48,256]{2,1,0:T(8,128)} copy(f32[16,48,256]{2,1,0:T(8,128)S(1)} %copy-done) | data formatting | bytes 1572864
Async XLA Ops:
  74.6 2.8 %copy-start.3 = (f32[32,16,256]{2,1,0:T(8,128)S(1)}, f32[32,16,256]{2,1,0:T(8,128)}, u32[]{:S(2)}) copy-start(f32[32,16,256]{2,1,0:T(8,128)} %get-tuple-element.11) | copy-start | bytes 1572868
  74.6 3.6 %copy-start.2 = (f32[32,16,256]{2,1,0:T(8,128)S(1)}, f32[32,16,256]{2,1,0:T(8,128)}, u32[]{:S(2)}) copy-start(f32[32,16,256]{2,1,0:T(8,128)} %get-tuple-element.12) | copy-start | bytes 1572868
  77.3 1.6 %copy-start.1 = (f32[32,16,256]{2,1,0:T(8,128)S(1)}, f32[32,16,256]{2,1,0:T(8,128)}, u32[]{:S(2)}) copy-start(f32[32,16,256]{2,1,0:T(8,128)} %get-tuple-element.13) | copy-start | bytes 1572868
  77.3 2.4 %copy-start = (f32[16,48,256]{2,1,0:T(8,128)S(1)}, f32[16,48,256]{2,1,0:T(8,128)}, u32[]{:S(2)}) copy-start(f32[16,48,256]{2,1,0:T(8,128)} %get-tuple-element.14) | copy-start | bytes 2359300

commit v3 on v2

--- a/solution.py
+++ b/solution.py
@@ -208,14 +208,34 @@
     return tiles
 
 
+PAIRS = (
+    (0, 0), (0, 1), (1, 0), (0, 3), (3, 0), (1, 1), (3, 3), (1, 3),
+    (3, 1), (0, 2), (2, 0), (2, 1), (1, 2), (2, 3), (3, 2), (2, 2),
+)
+LEAD = 7
+
+
 def peers():
     g, me = lax.axis_index("grid"), lax.axis_index("mark")
+    z, y = me // 4, lax.rem(me, 4)
+
+    def chosen(k, values):
+        if isinstance(k, int):
+            return values[k]
+        out = values[0]
+        for n in range(1, OWNERS):
+            out = jnp.where(k == n, values[n], out)
+        return out
 
     def after(k):
-        return lax.rem(me + k, OWNERS)
+        dz = chosen(k, [p[0] for p in PAIRS])
+        dy = chosen(k, [p[1] for p in PAIRS])
+        return lax.rem(z + dz, 4) * 4 + lax.rem(y + dy, 4)
 
     def before(k):
-        return lax.rem(me + OWNERS - k, OWNERS)
+        dz = chosen(k, [4 - p[0] for p in PAIRS])
+        dy = chosen(k, [4 - p[1] for p in PAIRS])
+        return lax.rem(z + dz, 4) * 4 + lax.rem(y + dy, 4)
 
     return g, me, after, before
 
@@ -228,15 +248,15 @@
 
 def step_kernel(
     counts, brick_ids, velocity, pressure, visc, dens, positions, start_visc, marker_dens,
-    velocity_out, pressure_out, visc_out, dens_out, marker_out,
+    velocity_out, pressure_out, marker_out, arrived, ids_out,
     state_a, state_b, visc_s, dens_s, halves, planes_hi, planes_lo, one_hot, ids_send, ids_recv,
     brick_send, bricks, kx, kym, kyp, kzm, kzp, damp, x_lo, x_hi, face_lo, face_hi, y_lo, y_hi,
-    vx_lo, vx_hi, vface_lo, vface_hi, vy_lo, vy_hi, pos, mvisc, mdens, marker_s, moments, arrived,
-    wz_s, wy_s, planes, hits, hi_s, lo_s, sums, cells,
+    vx_lo, vx_hi, vface_lo, vface_hi, vy_lo, vy_hi, pos, mvisc, mdens, marker_s, moments, wz_s, wy_s, planes,
     load_sem, id_send, id_recv, b_send, b_recv, h_send, h_recv, v_send, v_recv, m_send, m_recv, out_sem,
 ):
     g, me, after, before = peers()
     ahead, behind = lax.rem(g + 1, 8), lax.rem(g + 7, 8)
+    north, south = lax.rem(me + 1, OWNERS), lax.rem(me + OWNERS - 1, OWNERS)
     loads = [
         pltpu.make_async_copy(velocity, state_a.at[pl.ds(0, 3), pl.ds(1, NX_L)], load_sem.at[0]),
         pltpu.make_async_copy(pressure, state_a.at[3, pl.ds(1, NX_L)], load_sem.at[1]),
@@ -262,39 +282,40 @@
     ids_send[...] = jnp.full((OWNERS, 8, 128), -1.0, F32)
     for q in range(OWNERS):
         ids_send[q, :, pl.ds(0, CAP)] = jnp.broadcast_to(number[q : q + 1], (8, CAP))
-    pl.semaphore_wait(barrier, OWNERS + 1)
-
-    def send_ids(k, _):
-        remote(ids_send.at[after(k)], ids_recv.at[k], id_send.at[k], id_recv.at[k], (g, after(k))).start()
-        return 0
-
-    lax.fori_loop(1, OWNERS, send_ids, 0)
+
     ids_recv[0] = ids_send[me]
     for c in loads:
         c.wait()
 
+    def first_faces(x, _):
+        face_lo[0, x] = jnp.concatenate([state_a[c, x + 1, 0:1, :] for c in range(4)], axis=0)
+        face_hi[0, x] = jnp.concatenate([state_a[c, x + 1, 15:16, :] for c in range(4)], axis=0)
+        return 0
+
+    lax.fori_loop(0, NX_L, first_faces, 0, unroll=4)
+    for x in range(NX_L):
+        vface_lo[x : x + 1, :] = visc_s[x + 1, 0:1, :]
+        vface_hi[x : x + 1, :] = visc_s[x + 1, 15:16, :]
+    pl.semaphore_wait(barrier, OWNERS + 1)
+
+    def send_ids(k, _):
+        remote(ids_send.at[after(k)], ids_recv.at[k], id_send.at[k], id_recv.at[k], (g, after(k))).start()
+        return 0
+
+    lax.fori_loop(1, OWNERS, send_ids, 0)
     def halo(n, state):
         return [
             remote(state.at[:, 1], x_hi.at[n], h_send.at[n, 0], h_recv.at[n, 0], (behind, me)),
             remote(state.at[:, NX_L], x_lo.at[n], h_send.at[n, 1], h_recv.at[n, 1], (ahead, me)),
-            remote(face_lo.at[n], y_hi.at[n], h_send.at[n, 2], h_recv.at[n, 2], (g, before(1))),
-            remote(face_hi.at[n], y_lo.at[n], h_send.at[n, 3], h_recv.at[n, 3], (g, after(1))),
+            remote(face_lo.at[n], y_hi.at[n], h_send.at[n, 2], h_recv.at[n, 2], (g, south)),
+            remote(face_hi.at[n], y_lo.at[n], h_send.at[n, 3], h_recv.at[n, 3], (g, north)),
         ]
 
-    def first_faces(x, _):
-        face_lo[0, x] = jnp.concatenate([state_a[c, x + 1, 0:1, :] for c in range(4)], axis=0)
-        face_hi[0, x] = jnp.concatenate([state_a[c, x + 1, 15:16, :] for c in range(4)], axis=0)
-        return 0
-
-    lax.fori_loop(0, NX_L, first_faces, 0)
-    for x in range(NX_L):
-        vface_lo[x : x + 1, :] = visc_s[x + 1, 0:1, :]
-        vface_hi[x : x + 1, :] = visc_s[x + 1, 15:16, :]
     visc_halo = [
         remote(visc_s.at[1], vx_hi, v_send.at[0], v_recv.at[0], (behind, me)),
         remote(visc_s.at[NX_L], vx_lo, v_send.at[1], v_recv.at[1], (ahead, me)),
-        remote(vface_lo, vy_hi, v_send.at[2], v_recv.at[2], (g, before(1))),
-        remote(vface_hi, vy_lo, v_send.at[3], v_recv.at[3], (g, after(1))),
+        remote(vface_lo, vy_hi, v_send.at[2], v_recv.at[2], (g, south)),
+        remote(vface_hi, vy_lo, v_send.at[3], v_recv.at[3], (g, north)),
     ]
     for c in halo(0, state_a) + visc_halo:
         c.start()
@@ -307,7 +328,7 @@
                 halves[h, pl.ds(at, 16), :] = plane[:, 128 * h : 128 * h + 128]
         return 0
 
-    lax.fori_loop(0, NX_L, to_halves, 0)
+    lax.fori_loop(0, NX_L, to_halves, 0, unroll=2)
     group = lax.broadcasted_iota(jnp.int32, (8, 128), 1) // 8
 
     def to_bricks(n, _):
@@ -328,12 +349,6 @@
 
     lax.fori_loop(0, 8, to_bricks, 0)
 
-    def wait_ids(k, _):
-        remote(ids_send.at[after(k)], ids_recv.at[k], id_send.at[k], id_recv.at[k], (g, after(k))).wait()
-        return 0
-
-    lax.fori_loop(1, OWNERS, wait_ids, 0)
-
     def brick_copy(k):
         return remote(
             brick_send.at[k], bricks.at[k], b_send.at[k], b_recv.at[k], (g, before(k))
@@ -341,12 +356,15 @@
 
     lanes = lax.broadcasted_iota(jnp.int32, (CAP, 128), 1).astype(F32)
 
+    def hits_of(k, m):
+        column = jnp.transpose(jnp.broadcast_to(ids_recv[k][0:1, :], (128, 128)))[:CAP]
+        for t in range(8):
+            hit = jnp.where(column == lanes + 128.0 * t, 1.0, 0.0).astype(BF16)
+            one_hot[pl.ds(CAP * m, CAP), pl.ds(128 * t, 128)] = hit
+
     def gather(n, _):
         for m in range(4):
-            column = jnp.transpose(jnp.broadcast_to(ids_recv[4 * n + m][0:1, :], (128, 128)))[:CAP]
-            for t in range(8):
-                hit = jnp.where(column == lanes + 128.0 * t, 1.0, 0.0).astype(BF16)
-                one_hot[pl.ds(CAP * m, CAP), pl.ds(128 * t, 128)] = hit
+            hits_of(4 * n + m, m)
         found = jnp.dot(one_hot[...], planes_hi[...], preferred_element_type=F32)
         found = found + jnp.dot(one_hot[...], planes_lo[...], preferred_element_type=F32)
         for m in range(4):
@@ -354,14 +372,17 @@
         for m in range(4):
             k = 4 * n + m
 
-            @pl.when(k > 0)
+            @pl.when((k > 0) & (k <= LEAD))
             def _():
                 brick_copy(k).start()
 
         return 0
 
-    lax.fori_loop(0, 4, gather, 0)
-    bricks[0] = brick_send[0]
+    hits_of(0, 0)
+    own = one_hot[pl.ds(0, CAP), :]
+    bricks[0] = jnp.dot(own, planes_hi[...], preferred_element_type=F32) + jnp.dot(
+        own, planes_lo[...], preferred_element_type=F32
+    )
     for c in marker_loads:
         c.wait()
 
@@ -374,6 +395,10 @@
     def owner_markers(k, _):
         q = after(k)
         count = counts[0, q]
+
+        @pl.when((k > 0) & (k + LEAD < OWNERS))
+        def _():
+            brick_copy(k + LEAD).start()
 
         @pl.when(k > 0)
         def _():
@@ -398,6 +423,13 @@
         return 0
 
     lax.fori_loop(0, 1, owner_markers, 0)
+    def wait_ids(k, _):
+        remote(ids_send.at[after(k)], ids_recv.at[k], id_send.at[k], id_recv.at[k], (g, after(k))).wait()
+        return 0
+
+    lax.fori_loop(1, OWNERS, wait_ids, 0)
+
+    lax.fori_loop(0, 4, gather, 0)
 
     x_lo_on = (g > 0).astype(F32)
     x_hi_on = (g < 7).astype(F32)
@@ -440,7 +472,7 @@
         damp[x] = relax_weight / (k_xm + k_xp + k_ym + k_yp + k_zm + k_zp)
         return 0
 
-    lax.fori_loop(0, NX_L, couplings, 0)
+    lax.fori_loop(0, NX_L, couplings, 0, unroll=2)
 
     for n in range(SWEEPS):
         old, new = (state_a, state_b) if n % 2 == 0 else (state_b, state_a)
@@ -487,7 +519,7 @@
                 face_hi[n + 1, x] = jnp.concatenate([f[15:16] for f in fresh], axis=0)
             return 0
 
-        lax.fori_loop(0, NX_L, sweep, 0)
+        lax.fori_loop(0, NX_L, sweep, 0, unroll=2)
         if n + 1 < SWEEPS:
             for c in halo(n + 1, new):
                 c.start()
@@ -500,14 +532,47 @@
     ]
     for c in stores:
         c.start()
-    arrived[0] = moments[0]
-
+    own = pltpu.make_async_copy(moments.at[0], arrived.at[0], load_sem.at[9])
+    own.start()
+    ids_out[...] = ids_recv[...]
+
+    def arrive(k, _):
+        moment_copy(k).wait()
+        return 0
+
+    lax.fori_loop(1, OWNERS, arrive, 0)
+
+    def wait_markers(k, _):
+        marker_store(k).wait()
+        return 0
+
+    lax.fori_loop(0, OWNERS, wait_markers, 0)
+    own.wait()
+    for c in stores:
+        c.wait()
+
+
+def home_kernel(
+    moments, ids, visc, dens, velocity, pressure, markers,
+    visc_out, dens_out, velocity_out, pressure_out, markers_out,
+    arrived, visc_s, dens_s, velocity_s, pressure_s, markers_s, hits, hi_s, lo_s, sums, cells, sem,
+):
+    loads = [
+        pltpu.make_async_copy(moments, arrived, sem.at[0]),
+        pltpu.make_async_copy(visc, visc_s, sem.at[1]),
+        pltpu.make_async_copy(dens, dens_s, sem.at[2]),
+    ]
+    stages = ((velocity, velocity_s, velocity_out), (pressure, pressure_s, pressure_out), (markers, markers_s, markers_out))
+    fetches = [pltpu.make_async_copy(a, b, sem.at[3 + n]) for n, (a, b, c) in enumerate(stages)]
+    copies = [pltpu.make_async_copy(b, c, sem.at[6 + n]) for n, (a, b, c) in enumerate(stages)]
+    for c in loads + fetches:
+        c.start()
     lane = lax.broadcasted_iota(jnp.int32, (8, 128), 1)
     rows = [jnp.full((8, 128), -1.0, F32) for _ in range(6)]
     for k in range(OWNERS):
         at = CAP * k
         t, off = at // 128, at % 128
-        tile = ids_recv[k]
+        tile = ids[k]
         turned = pltpu.roll(tile, off, 1) if off else tile
         rows[t] = jnp.where((lane >= off) & (lane < off + CAP), turned, rows[t])
         over = off + CAP - 128
@@ -524,13 +589,10 @@
             hits[pl.ds(at, 16), pl.ds(128 * t, 128)] = jnp.where(wide[t] == here, 1.0, 0.0).astype(BF16)
         return 0
 
-    lax.fori_loop(0, BRICKS // 16, mark_hits, 0)
-
-    def arrive(k, _):
-        moment_copy(k).wait()
-        return 0
-
-    lax.fori_loop(1, OWNERS, arrive, 0)
+    lax.fori_loop(0, BRICKS // 16, mark_hits, 0, unroll=4)
+
+    for c in loads:
+        c.wait()
 
     def moment_pieces(k, _):
         hi, lo = split(arrived[k])
@@ -550,7 +612,12 @@
             sums[m, at, :] = total[:, 128 * m : 128 * m + 128]
         return 0
 
+    for fetch, c in zip(fetches, copies):
+        fetch.wait()
+        c.start()
     lax.fori_loop(0, 4, scatter, 0)
+    group = lane // 8
+
     def to_cells(n, _):
         bj, h = n // 2, lax.rem(n, 2)
         for m in range(3):
@@ -570,18 +637,12 @@
         for h in range(2):
             part = pl.ds(128 * h, 128)
             below = 1.0 / (cells[0, h, at, :] + 1.0)
-            visc_out[x, :, part] = jnp.exp((cells[1, h, at, :] + jnp.log(visc_s[x + 1, :, part])) * below)
+            visc_out[x, :, part] = jnp.exp((cells[1, h, at, :] + jnp.log(visc_s[x, :, part])) * below)
             dens_out[x, :, part] = (cells[2, h, at, :] + dens_s[x, :, part]) * below
         return 0
 
-    lax.fori_loop(0, NX_L, finish, 0)
-
-    def wait_markers(k, _):
-        marker_store(k).wait()
-        return 0
-
-    lax.fori_loop(0, OWNERS, wait_markers, 0)
-    for c in stores:
+    lax.fori_loop(0, NX_L, finish, 0, unroll=2)
+    for c in copies:
         c.wait()
 
 
@@ -594,17 +655,17 @@
     field = (NX_L, NY_L, NZ)
     padded = (NX_L + 2, NY_L, NZ)
     shape = jax.ShapeDtypeStruct
-    return pl.pallas_call(
+    velocity_next, pressure_next, markers, moments, ids = pl.pallas_call(
         step_kernel,
         out_shape=(
             shape((3,) + field, F32),
             shape(field, F32),
-            shape(field, F32),
-            shape(field, F32),
             shape((OWNERS, CAP, BLOCK), F32),
+            shape((OWNERS, CAP, 384), F32),
+            shape((OWNERS, 8, 128), F32),
         ),
         in_specs=[pl.BlockSpec(memory_space=pltpu.SMEM), vm] + [hbm] * 7,
-        out_specs=(hbm, hbm, vm, vm, hbm),
+        out_specs=(hbm, hbm, hbm, hbm, vm),
         scratch_shapes=[
             VMEM((4,) + padded, F32),
             VMEM((4,) + padded, F32),
@@ -641,16 +702,10 @@
             VMEM((OWNERS, CAP, BLOCK), F32),
             VMEM((OWNERS, CAP, BLOCK), F32),
             VMEM((OWNERS, CAP, 384), F32),
-            VMEM((OWNERS, CAP, 384), F32),
             VMEM((GROUPS, 2, 64, 128), F32),
             VMEM((GROUPS, 2, 32, 128), F32),
             VMEM((GROUPS, 2, 256, 256), BF16),
-            VMEM((BRICKS, OWNERS * CAP), BF16),
-            VMEM((OWNERS * CAP, 384), BF16),
-            VMEM((OWNERS * CAP, 384), BF16),
-            VMEM((3, BRICKS, 128), F32),
-            VMEM((3, 2, 512, 128), F32),
-            dma((9,)),
+            dma((10,)),
             dma((OWNERS,)),
             dma((OWNERS,)),
             dma((OWNERS,)),
@@ -671,6 +726,35 @@
         block_counts, block_brick, velocity, pressure, cell_visc, cell_dens,
         positions, start_visc, marker_dens,
     )
+    visc_next, dens_next, velocity_next, pressure_next, markers = pl.pallas_call(
+        home_kernel,
+        out_shape=(
+            shape(field, F32),
+            shape(field, F32),
+            shape((3,) + field, F32),
+            shape(field, F32),
+            shape((OWNERS, CAP, BLOCK), F32),
+        ),
+        in_specs=[hbm, vm] + [hbm] * 5,
+        out_specs=(vm, vm, hbm, hbm, hbm),
+        scratch_shapes=[
+            VMEM((OWNERS, CAP, 384), F32),
+            VMEM(field, F32),
+            VMEM(field, F32),
+            VMEM((3,) + field, F32),
+            VMEM(field, F32),
+            VMEM((OWNERS, CAP, BLOCK), F32),
+            VMEM((BRICKS, OWNERS * CAP), BF16),
+            VMEM((OWNERS * CAP, 384), BF16),
+            VMEM((OWNERS * CAP, 384), BF16),
+            VMEM((3, BRICKS, 128), F32),
+            VMEM((3, 2, 512, 128), F32),
+            dma((9,)),
+        ],
+        compiler_params=pltpu.CompilerParams(vmem_limit_bytes=56 << 20),
+        name="home",
+    )(moments, ids, cell_visc, cell_dens, velocity_next, pressure_next, markers)
+    return velocity_next, pressure_next, visc_next, dens_next, markers
 
 
 def solution(mesh):

time: 81.9 us -> 71.7 us (0.88)
  local copies, waits for them, and re-layouts: 6.03 us -> 0 us
  Pallas kernels: 73.9 us -> 69.7 us
    pallas_call x1, Pallas kernels: 73.9 us -> 59.5 us  [per_device(): pl.pallas_call(step_kernel, out_shape=(shape((3,) + field, F32), shape(fi...]
    pallas_call x0 -> x1, Pallas kernels: none -> 10.2 us  [per_device(): pl.pallas_call(home_kernel, out_shape=(shape(field, F32), shape(field, F3...]
    unnamed x13 -> x0, local copies, waits for them, and re-layouts: 6.03 us -> none
where the time goes in v3:
time: 71.7 us; the launch traced here: 70.3 us
  Pallas kernels  69.7 us (97%)
    pallas_call x1, Pallas kernels, per_device(): pl.pallas_call(step_kernel, out_shape=(shape((3,) + field, F32), shape(fi...  59.5 us
    pallas_call x1, Pallas kernels, per_device(): pl.pallas_call(home_kernel, out_shape=(shape(field, F32), shape(field, F3...  10.2 us

profile of v3, /device:TPU:38, one launch (start us, length us, event | category | flops | bytes accessed | tf_op | source)
XLA Modules:
  0.0 70.3 jit_solution(8716913391388996098)
XLA Ops:
  0.6 59.5 %step.1 = (f32[3,32,16,256]{3,2,1,0:T(8,128)}, f32[32,16,256]{2,1,0:T(8,128)}, f32[16,48,256]{2,1,0:T(8,128)}, f32[16,48,384]{2,1,0:T(8,128)}, f32[16,8,128]{2,1,0:T(8,128)}) custom-call(s32[1,16]{1,0:T(1,128)} %counts.1, s32[16,48]{1,0:T(8,128)} %brick_ids.1, f32[3,32,16,256]{3,2,1,0:T(8,128)} %velocity.1, f32[32,16,256]{2,1,0:T(8,128)} %pressure.1, ...), custom_call_target="tpu_custom_call" | custom-call | tf_op jit(solution)/shard_map/step/pallas_call | solution.py:658
  60.1 10.2 %home.1 = (f32[32,16,256]{2,1,0:T(8,128)}, f32[32,16,256]{2,1,0:T(8,128)}, f32[3,32,16,256]{3,2,1,0:T(8,128)}, f32[32,16,256]{2,1,0:T(8,128)}, f32[16,48,256]{2,1,0:T(8,128)}) custom-call(f32[16,48,384]{2,1,0:T(8,128)} %get-tuple-element.15.moments, f32[16,8,128]{2,1,0:T(8,128)} %get-tuple-element.16.ids, f32[32,16,256]{2,1,0:T(8,128)} %visc.3, ...), custom_call_target="tpu_custom_call" | custom-call | tf_op jit(solution)/shard_map/home/pallas_call | solution.py:729

commit v4 on v3

--- a/solution.py
+++ b/solution.py
@@ -405,13 +405,13 @@
             brick_copy(k).wait()
 
         ready, spread = {}, {}
-        for t in range(GROUPS + 2):
+        for t in range(GROUPS + 4):
             if t < GROUPS:
                 ready[t] = prepare(q, k, 8 * t, t, pos, bricks, wz_s, wy_s, planes)
-            u = t - 1
+            u = t - 2
             if 0 <= u < GROUPS:
                 spread[u] = strain(q, k, 8 * u, u, ready.pop(u), mvisc, mdens, marker_s, count, planes)
-            u = t - 2
+            u = t - 4
             if 0 <= u < GROUPS:
                 deposit(k, 8 * u, u, spread.pop(u), moments, planes)
         marker_store(k).start()
@@ -603,34 +603,33 @@
 
     lax.fori_loop(0, OWNERS, moment_pieces, 0)
 
-    def scatter(n, _):
-        at = pl.ds(pl.multiple_of(n * 256, 256), 256)
+    group = lane // 8
+
+    def scatter(n):
+        at = pl.ds(256 * n, 256)
         block = hits[at, :]
         total = jnp.dot(block, hi_s[...], preferred_element_type=F32)
         total = total + jnp.dot(block, lo_s[...], preferred_element_type=F32)
         for m in range(3):
             sums[m, at, :] = total[:, 128 * m : 128 * m + 128]
-        return 0
+
+    def to_cells(bj):
+        for h in range(2):
+            for m in range(3):
+                tiles = [sums[m, pl.ds((bj * 32 + h * 16 + t) * 8, 8), :] for t in range(16)]
+                tiles = group_transpose(tiles, group)
+                for i in range(4):
+                    for j in range(4):
+                        cells[m, h, pl.ds(16 * i + 4 * bj + j, 8, stride=64), :] = tiles[4 * i + j]
 
     for fetch, c in zip(fetches, copies):
         fetch.wait()
         c.start()
-    lax.fori_loop(0, 4, scatter, 0)
-    group = lane // 8
-
-    def to_cells(n, _):
-        bj, h = n // 2, lax.rem(n, 2)
-        for m in range(3):
-            tiles = [
-                sums[m, pl.ds(pl.multiple_of((bj * 32 + h * 16 + t) * 8, 8), 8), :] for t in range(16)
-            ]
-            tiles = group_transpose(tiles, group)
-            for i in range(4):
-                for j in range(4):
-                    cells[m, h, pl.ds(16 * i + 4 * bj + j, 8, stride=64), :] = tiles[4 * i + j]
-        return 0
-
-    lax.fori_loop(0, 8, to_cells, 0)
+    scatter(0)
+    for n in range(4):
+        if n < 3:
+            scatter(n + 1)
+        to_cells(n)
 
     def finish(x, _):
         at = pl.ds(pl.multiple_of(x * 16, 16), 16)

time: 71.7 us -> 67.7 us (0.944)
  Pallas kernels: 69.7 us -> 65.7 us
    pallas_call x1, Pallas kernels: 10.2 us -> 7.75 us  [per_device(): pl.pallas_call(home_kernel, out_shape=(shape(field, F32), shape(field, F3...]
    pallas_call x1, Pallas kernels: 59.5 us -> 57.9 us  [per_device(): pl.pallas_call(step_kernel, out_shape=(shape((3,) + field, F32), shape(fi...]
where the time goes in v4:
time: 67.7 us; the launch traced here: 66.3 us
  Pallas kernels  65.7 us (97%)
    pallas_call x1, Pallas kernels, per_device(): pl.pallas_call(step_kernel, out_shape=(shape((3,) + field, F32), shape(fi...  57.9 us
    pallas_call x1, Pallas kernels, per_device(): pl.pallas_call(home_kernel, out_shape=(shape(field, F32), shape(field, F3...  7.75 us

profile of v4, /device:TPU:38, one launch (start us, length us, event | category | flops | bytes accessed | tf_op | source)
XLA Modules:
  0.0 66.3 jit_solution(14240411834365749756)
XLA Ops:
  0.6 57.9 %step.1 = (f32[3,32,16,256]{3,2,1,0:T(8,128)}, f32[32,16,256]{2,1,0:T(8,128)}, f32[16,48,256]{2,1,0:T(8,128)}, f32[16,48,384]{2,1,0:T(8,128)}, f32[16,8,128]{2,1,0:T(8,128)}) custom-call(s32[1,16]{1,0:T(1,128)} %counts.1, s32[16,48]{1,0:T(8,128)} %brick_ids.1, f32[3,32,16,256]{3,2,1,0:T(8,128)} %velocity.1, f32[32,16,256]{2,1,0:T(8,128)} %pressure.1, ...), custom_call_target="tpu_custom_call" | custom-call | tf_op jit(solution)/shard_map/step/pallas_call | solution.py:657
  58.6 7.8 %home.1 = (f32[32,16,256]{2,1,0:T(8,128)}, f32[32,16,256]{2,1,0:T(8,128)}, f32[3,32,16,256]{3,2,1,0:T(8,128)}, f32[32,16,256]{2,1,0:T(8,128)}, f32[16,48,256]{2,1,0:T(8,128)}) custom-call(f32[16,48,384]{2,1,0:T(8,128)} %get-tuple-element.15.moments, f32[16,8,128]{2,1,0:T(8,128)} %get-tuple-element.16.ids, f32[32,16,256]{2,1,0:T(8,128)} %visc.3, ...), custom_call_target="tpu_custom_call" | custom-call | tf_op jit(solution)/shard_map/home/pallas_call | solution.py:728

commit v5 on v4

--- a/solution.py
+++ b/solution.py
@@ -21,7 +21,8 @@
 
 def axis_weights(fraction, cells):
     half = 0.5 * cells
-    factor = jnp.exp(2.0 * cells * fraction - 2.0 * half)
+    turn = 2.0 / math.log(2.0)
+    factor = jnp.exp2((turn * cells) * fraction - turn * half)
     centres = [i + 0.5 - half for i in range(cells)]
     powers = [None, factor]
     for i in range(2, cells):
@@ -31,7 +32,9 @@
     total = functools.reduce(jnp.add, raw)
     scale = 1.0 / total
     weights = [r * scale for r in raw]
-    mean = functools.reduce(jnp.add, [c * w for c, w in zip(centres, weights)])
+    mean = functools.reduce(
+        jnp.add, [centres[-1 - n] * (weights[-1 - n] - weights[n]) for n in range(cells // 2)]
+    )
     return weights, mean
 
 
@@ -98,6 +101,10 @@
     c_j = ((lane // 8) % 4).astype(F32) - 1.5
     c_k = (lane % 8).astype(F32) - 3.5
     v = [both(skew(bricks[k, rows, pl.ds(128 * c, 128)], sub, 1), low) for c in range(3)]
+    sub16 = lax.broadcasted_iota(jnp.int32, (16, 128), 0)
+    lane16 = lax.broadcasted_iota(jnp.int32, (16, 128), 1)
+    low16 = sub16 % 8 < 4
+    diag16 = (lane16 // 32) == (sub16 % 4)
     lefts = []
     for side in range(2):
         vx, vy, vz = [x[side] for x in v]
@@ -105,13 +112,18 @@
             vx, vy, vz, c_j * vy, c_k * vz,
             c_j * vx + c_i * vy, c_k * vx + c_i * vz, c_k * vy + c_j * vz,
         ]
-        tiles = []
-        for kind in kinds:
-            turned = [kind] + [pltpu.roll(kind, 128 - 32 * i, 1) for i in range(1, 4)]
-            for ip in range(2):
-                tile = jnp.where(low, turned[2 * ip], turned[2 * ip + 1])
-                tiles.append(jnp.where(diag, tile, 0.0))
-        lefts.append(pieces(tiles))
+        parts = []
+        for n in range(0, 8, 2):
+            parts.append(split(jnp.concatenate(kinds[n : n + 2], axis=0)))
+        left = []
+        for piece in range(2):
+            for part in parts:
+                src = part[piece]
+                turned = [src] + [pltpu.roll(src, 128 - 32 * i, 1) for i in range(1, 4)]
+                for ip in range(2):
+                    tile = jnp.where(low16, turned[2 * ip], turned[2 * ip + 1])
+                    left.append(jnp.where(diag16, tile, jnp.zeros_like(tile)))
+        lefts.append(jnp.concatenate(left, axis=0))
     pairs = ([], [])
     for ip in range(2):
         first, second = both(wx[2 * ip], low2), both(wx[2 * ip + 1], low2)
@@ -135,10 +147,10 @@
     ]
 
     def along_x(kind, weights):
-        at = 16 * kind
+        at = 32 * (kind // 2) + 8 * (kind % 2)
         sums = [
             results[side][at : at + 8] * weights[side][0]
-            + results[side][at + 8 : at + 16] * weights[side][1]
+            + results[side][at + 16 : at + 24] * weights[side][1]
             for side in range(2)
         ]
         return fold(*sums, low2)
@@ -151,14 +163,14 @@
     xz = xz - mean_z * vx - mean_x * vz
     yz = yz - mean_z * vy - mean_y * vz
     invariant = 2.0 * (xx * xx + yy * yy + zz * zz) + xy * xy + xz * xz + yz * yz
-    shift = jnp.log(1.0 + invariant * 4.0) * (1.0 / 3.0)
+    shift = jnp.log2(1.0 + invariant * 4.0) * (-1.0 / 3.0)
     start = visc[q, rows, :]
     live = (sub2 + row) < count
-    weakened = start * jnp.exp(-shift)
+    weakened = start * jnp.exp2(shift)
     marker_out[k, rows, :] = jnp.where(live, weakened, 0.0)
     carried = [
         jnp.where(live, 1.0, 0.0),
-        jnp.where(live, jnp.log(weakened), 0.0),
+        jnp.where(live, math.log(2.0) * (jnp.log2(start) + shift), 0.0),
         jnp.where(live, dens[q, rows, :], 0.0),
     ]
     carried = [both(c, low2) for c in carried]
@@ -247,9 +259,9 @@
 
 
 def step_kernel(
-    counts, brick_ids, velocity, pressure, visc, dens, positions, start_visc, marker_dens,
+    counts, ids_in, velocity, pressure, visc, dens, positions, start_visc, marker_dens,
     velocity_out, pressure_out, marker_out, arrived, ids_out,
-    state_a, state_b, visc_s, dens_s, halves, planes_hi, planes_lo, one_hot, ids_send, ids_recv,
+    brick_ids, state_a, state_b, visc_s, dens_s, halves, planes_hi, planes_lo, one_hot, ids_send, ids_recv,
     brick_send, bricks, kx, kym, kyp, kzm, kzp, damp, x_lo, x_hi, face_lo, face_hi, y_lo, y_hi,
     vx_lo, vx_hi, vface_lo, vface_hi, vy_lo, vy_hi, pos, mvisc, mdens, marker_s, moments, wz_s, wy_s, planes,
     load_sem, id_send, id_recv, b_send, b_recv, h_send, h_recv, v_send, v_recv, m_send, m_recv, out_sem,
@@ -263,6 +275,8 @@
         pltpu.make_async_copy(visc, visc_s.at[pl.ds(1, NX_L)], load_sem.at[2]),
         pltpu.make_async_copy(dens, dens_s, load_sem.at[3]),
     ]
+    ids_load = pltpu.make_async_copy(ids_in, brick_ids, load_sem.at[10])
+    ids_load.start()
     marker_loads = [
         pltpu.make_async_copy(positions, pos, load_sem.at[4]),
         pltpu.make_async_copy(start_visc, mvisc, load_sem.at[7]),
@@ -276,6 +290,7 @@
     pl.semaphore_signal(barrier, inc=1, device_id=(ahead, me), device_id_type=MESH)
     pl.semaphore_signal(barrier, inc=1, device_id=(behind, me), device_id_type=MESH)
 
+    ids_load.wait()
     number = brick_ids[...]
     number = (((number >> 5) & 3) * 32 + (number & 31)) * 8 + (number >> 7)
     number = number.astype(F32)
@@ -429,6 +444,8 @@
 
     lax.fori_loop(1, OWNERS, wait_ids, 0)
 
+    ids_store = pltpu.make_async_copy(ids_recv, ids_out, load_sem.at[11])
+    ids_store.start()
     lax.fori_loop(0, 4, gather, 0)
 
     x_lo_on = (g > 0).astype(F32)
@@ -519,7 +536,7 @@
                 face_hi[n + 1, x] = jnp.concatenate([f[15:16] for f in fresh], axis=0)
             return 0
 
-        lax.fori_loop(0, NX_L, sweep, 0, unroll=2)
+        lax.fori_loop(0, NX_L, sweep, 0, unroll=4)
         if n + 1 < SWEEPS:
             for c in halo(n + 1, new):
                 c.start()
@@ -534,7 +551,6 @@
         c.start()
     own = pltpu.make_async_copy(moments.at[0], arrived.at[0], load_sem.at[9])
     own.start()
-    ids_out[...] = ids_recv[...]
 
     def arrive(k, _):
         moment_copy(k).wait()
@@ -548,14 +564,15 @@
 
     lax.fori_loop(0, OWNERS, wait_markers, 0)
     own.wait()
+    ids_store.wait()
     for c in stores:
         c.wait()
 
 
 def home_kernel(
-    moments, ids, visc, dens, velocity, pressure, markers,
+    moments, ids_in, visc, dens, velocity, pressure, markers,
     visc_out, dens_out, velocity_out, pressure_out, markers_out,
-    arrived, visc_s, dens_s, velocity_s, pressure_s, markers_s, hits, hi_s, lo_s, sums, cells, sem,
+    ids, visc_new, dens_new, arrived, visc_s, dens_s, velocity_s, pressure_s, markers_s, hits, hi_s, lo_s, sums, cells, sem,
 ):
     loads = [
         pltpu.make_async_copy(moments, arrived, sem.at[0]),
@@ -565,8 +582,10 @@
     stages = ((velocity, velocity_s, velocity_out), (pressure, pressure_s, pressure_out), (markers, markers_s, markers_out))
     fetches = [pltpu.make_async_copy(a, b, sem.at[3 + n]) for n, (a, b, c) in enumerate(stages)]
     copies = [pltpu.make_async_copy(b, c, sem.at[6 + n]) for n, (a, b, c) in enumerate(stages)]
-    for c in loads + fetches:
+    ids_load = pltpu.make_async_copy(ids_in, ids, sem.at[9])
+    for c in [ids_load] + loads + fetches:
         c.start()
+    ids_load.wait()
     lane = lax.broadcasted_iota(jnp.int32, (8, 128), 1)
     rows = [jnp.full((8, 128), -1.0, F32) for _ in range(6)]
     for k in range(OWNERS):
@@ -601,7 +620,7 @@
         lo_s[pl.ds(at, CAP), :] = lo
         return 0
 
-    lax.fori_loop(0, OWNERS, moment_pieces, 0)
+    lax.fori_loop(0, OWNERS, moment_pieces, 0, unroll=4)
 
     group = lane // 8
 
@@ -636,11 +655,17 @@
         for h in range(2):
             part = pl.ds(128 * h, 128)
             below = 1.0 / (cells[0, h, at, :] + 1.0)
-            visc_out[x, :, part] = jnp.exp((cells[1, h, at, :] + jnp.log(visc_s[x, :, part])) * below)
-            dens_out[x, :, part] = (cells[2, h, at, :] + dens_s[x, :, part]) * below
-        return 0
-
-    lax.fori_loop(0, NX_L, finish, 0, unroll=2)
+            visc_new[x, :, part] = jnp.exp((cells[1, h, at, :] + jnp.log(visc_s[x, :, part])) * below)
+            dens_new[x, :, part] = (cells[2, h, at, :] + dens_s[x, :, part]) * below
+        return 0
+
+    for n in range(4):
+        lax.fori_loop(8 * n, 8 * n + 8, finish, 0, unroll=2)
+        part = pl.ds(8 * n, 8)
+        for m, (new, out) in enumerate(((visc_new, visc_out), (dens_new, dens_out))):
+            c = pltpu.make_async_copy(new.at[part], out.at[part], sem.at[10 + 2 * n + m])
+            c.start()
+            copies.append(c)
     for c in copies:
         c.wait()
 
@@ -648,7 +673,6 @@
 def per_device(
     velocity, pressure, cell_visc, cell_dens, block_brick, block_counts, positions, start_visc, marker_dens
 ):
-    vm = pl.BlockSpec(memory_space=pltpu.VMEM)
     hbm = pl.BlockSpec(memory_space=pl.ANY)
     dma = pltpu.SemaphoreType.DMA
     field = (NX_L, NY_L, NZ)
@@ -663,9 +687,10 @@
             shape((OWNERS, CAP, 384), F32),
             shape((OWNERS, 8, 128), F32),
         ),
-        in_specs=[pl.BlockSpec(memory_space=pltpu.SMEM), vm] + [hbm] * 7,
-        out_specs=(hbm, hbm, hbm, hbm, vm),
+        in_specs=[pl.BlockSpec(memory_space=pltpu.SMEM)] + [hbm] * 8,
+        out_specs=(hbm,) * 5,
         scratch_shapes=[
+            VMEM((OWNERS, CAP), jnp.int32),
             VMEM((4,) + padded, F32),
             VMEM((4,) + padded, F32),
             VMEM(padded, F32),
@@ -704,7 +729,7 @@
             VMEM((GROUPS, 2, 64, 128), F32),
             VMEM((GROUPS, 2, 32, 128), F32),
             VMEM((GROUPS, 2, 256, 256), BF16),
-            dma((10,)),
+            dma((12,)),
             dma((OWNERS,)),
             dma((OWNERS,)),
             dma((OWNERS,)),
@@ -734,9 +759,12 @@
             shape(field, F32),
             shape((OWNERS, CAP, BLOCK), F32),
         ),
-        in_specs=[hbm, vm] + [hbm] * 5,
-        out_specs=(vm, vm, hbm, hbm, hbm),
+        in_specs=[hbm] * 7,
+        out_specs=(hbm,) * 5,
         scratch_shapes=[
+            VMEM((OWNERS, 8, 128), F32),
+            VMEM(field, F32),
+            VMEM(field, F32),
             VMEM((OWNERS, CAP, 384), F32),
             VMEM(field, F32),
             VMEM(field, F32),
@@ -748,7 +776,7 @@
             VMEM((OWNERS * CAP, 384), BF16),
             VMEM((3, BRICKS, 128), F32),
             VMEM((3, 2, 512, 128), F32),
-            dma((9,)),
+            dma((18,)),
         ],
         compiler_params=pltpu.CompilerParams(vmem_limit_bytes=56 << 20),
         name="home",

time: 67.7 us -> 65.6 us (0.969)
  Pallas kernels: 65.7 us -> 63.7 us
    pallas_call x1, Pallas kernels: 57.9 us -> 56.9 us  [per_device(): pl.pallas_call(step_kernel, out_shape=(shape((3,) + field, F32), shape(fi...]
    pallas_call x1, Pallas kernels: 7.75 us -> 6.76 us  [per_device(): pl.pallas_call(home_kernel, out_shape=(shape(field, F32), shape(field, F3...]
where the time goes in v5:
time: 65.6 us; the launch traced here: 64.3 us
  Pallas kernels  63.7 us (97%)
    pallas_call x1, Pallas kernels, per_device(): pl.pallas_call(step_kernel, out_shape=(shape((3,) + field, F32), shape(fi...  56.9 us
    pallas_call x1, Pallas kernels, per_device(): pl.pallas_call(home_kernel, out_shape=(shape(field, F32), shape(field, F3...  6.76 us

profile of v5, /device:TPU:38, one launch (start us, length us, event | category | flops | bytes accessed | tf_op | source)
XLA Modules:
  0.0 64.3 jit_solution(6123829014389296624)
XLA Ops:
  0.6 56.9 %step.1 = (f32[3,32,16,256]{3,2,1,0:T(8,128)}, f32[32,16,256]{2,1,0:T(8,128)}, f32[16,48,256]{2,1,0:T(8,128)}, f32[16,48,384]{2,1,0:T(8,128)}, f32[16,8,128]{2,1,0:T(8,128)}) custom-call(s32[1,16]{1,0:T(1,128)} %counts.1, s32[16,48]{1,0:T(8,128)} %ids_in.1, f32[3,32,16,256]{3,2,1,0:T(8,128)} %velocity.1, f32[32,16,256]{2,1,0:T(8,128)} %pressure.1, ...), custom_call_target="tpu_custom_call" | custom-call | tf_op jit(solution)/shard_map/step/pallas_call | solution.py:681
  57.6 6.8 %home.1 = (f32[32,16,256]{2,1,0:T(8,128)}, f32[32,16,256]{2,1,0:T(8,128)}, f32[3,32,16,256]{3,2,1,0:T(8,128)}, f32[32,16,256]{2,1,0:T(8,128)}, f32[16,48,256]{2,1,0:T(8,128)}) custom-call(f32[16,48,384]{2,1,0:T(8,128)} %get-tuple-element.15.moments, f32[16,8,128]{2,1,0:T(8,128)} %get-tuple-element.16.ids_in, f32[32,16,256]{2,1,0:T(8,128)} %visc.3, ...), custom_call_target="tpu_custom_call" | custom-call | tf_op jit(solution)/shard_map/home/pallas_call | solution.py:753

commit v6 on v5

--- a/solution.py
+++ b/solution.py
@@ -343,7 +343,7 @@
                 halves[h, pl.ds(at, 16), :] = plane[:, 128 * h : 128 * h + 128]
         return 0
 
-    lax.fori_loop(0, NX_L, to_halves, 0, unroll=2)
+    lax.fori_loop(0, NX_L, to_halves, 0, unroll=4)
     group = lax.broadcasted_iota(jnp.int32, (8, 128), 1) // 8
 
     def to_bricks(n, _):
@@ -362,7 +362,7 @@
                 planes_lo[pl.ds(at, 16), pl.ds(128 * c, 128)] = lo
         return 0
 
-    lax.fori_loop(0, 8, to_bricks, 0)
+    lax.fori_loop(0, 8, to_bricks, 0, unroll=2)
 
     def brick_copy(k):
         return remote(
@@ -378,14 +378,14 @@
             one_hot[pl.ds(CAP * m, CAP), pl.ds(128 * t, 128)] = hit
 
     def gather(n, _):
-        for m in range(4):
-            hits_of(4 * n + m, m)
+        for m in range(8):
+            hits_of(8 * n + m, m)
         found = jnp.dot(one_hot[...], planes_hi[...], preferred_element_type=F32)
         found = found + jnp.dot(one_hot[...], planes_lo[...], preferred_element_type=F32)
-        for m in range(4):
-            brick_send[4 * n + m] = found[CAP * m : CAP * m + CAP]
-        for m in range(4):
-            k = 4 * n + m
+        for m in range(8):
+            brick_send[8 * n + m] = found[CAP * m : CAP * m + CAP]
+        for m in range(8):
+            k = 8 * n + m
 
             @pl.when((k > 0) & (k <= LEAD))
             def _():
@@ -446,7 +446,7 @@
 
     ids_store = pltpu.make_async_copy(ids_recv, ids_out, load_sem.at[11])
     ids_store.start()
-    lax.fori_loop(0, 4, gather, 0)
+    lax.fori_loop(0, 2, gather, 0)
 
     x_lo_on = (g > 0).astype(F32)
     x_hi_on = (g < 7).astype(F32)
@@ -489,7 +489,7 @@
         damp[x] = relax_weight / (k_xm + k_xp + k_ym + k_yp + k_zm + k_zp)
         return 0
 
-    lax.fori_loop(0, NX_L, couplings, 0, unroll=2)
+    lax.fori_loop(0, NX_L, couplings, 0, unroll=4)
 
     for n in range(SWEEPS):
         old, new = (state_a, state_b) if n % 2 == 0 else (state_b, state_a)
@@ -698,7 +698,7 @@
             VMEM((2, 1536, 128), F32),
             VMEM((BRICKS, 384), BF16),
             VMEM((BRICKS, 384), BF16),
-            VMEM((4 * CAP, BRICKS), BF16),
+            VMEM((8 * CAP, BRICKS), BF16),
             VMEM((OWNERS, 8, 128), F32),
             VMEM((OWNERS, 8, 128), F32),
             VMEM((OWNERS, CAP, 384), F32),

time: 65.6 us -> 64.8 us (0.988)
  Pallas kernels: 63.7 us -> 62.8 us
    pallas_call x1, Pallas kernels: 56.9 us -> 56 us  [per_device(): pl.pallas_call(step_kernel, out_shape=(shape((3,) + field, F32), shape(fi...]
where the time goes in v6:
time: 64.8 us; the launch traced here: 63.6 us
  Pallas kernels  62.8 us (97%)
  between operations  0.8 us (1%)
    pallas_call x1, Pallas kernels, per_device(): pl.pallas_call(step_kernel, out_shape=(shape((3,) + field, F32), shape(fi...  56 us
    pallas_call x1, Pallas kernels, per_device(): pl.pallas_call(home_kernel, out_shape=(shape(field, F32), shape(field, F3...  6.76 us

profile of v6, /device:TPU:38, one launch (start us, length us, event | category | flops | bytes accessed | tf_op | source)
XLA Modules:
  0.0 63.6 jit_solution(16770447106985188170)
XLA Ops:
  0.6 56.0 %step.1 = (f32[3,32,16,256]{3,2,1,0:T(8,128)}, f32[32,16,256]{2,1,0:T(8,128)}, f32[16,48,256]{2,1,0:T(8,128)}, f32[16,48,384]{2,1,0:T(8,128)}, f32[16,8,128]{2,1,0:T(8,128)}) custom-call(s32[1,16]{1,0:T(1,128)} %counts.1, s32[16,48]{1,0:T(8,128)} %ids_in.1, f32[3,32,16,256]{3,2,1,0:T(8,128)} %velocity.1, f32[32,16,256]{2,1,0:T(8,128)} %pressure.1, ...), custom_call_target="tpu_custom_call" | custom-call | tf_op jit(solution)/shard_map/step/pallas_call | solution.py:681
  56.6 6.8 %home.1 = (f32[32,16,256]{2,1,0:T(8,128)}, f32[32,16,256]{2,1,0:T(8,128)}, f32[3,32,16,256]{3,2,1,0:T(8,128)}, f32[32,16,256]{2,1,0:T(8,128)}, f32[16,48,256]{2,1,0:T(8,128)}) custom-call(f32[16,48,384]{2,1,0:T(8,128)} %get-tuple-element.15.moments, f32[16,8,128]{2,1,0:T(8,128)} %get-tuple-element.16.ids_in, f32[32,16,256]{2,1,0:T(8,128)} %visc.3, ...), custom_call_target="tpu_custom_call" | custom-call | tf_op jit(solution)/shard_map/home/pallas_call | solution.py:753
